TPU v7x, 256 devices: a whole 4x4x8 slice. The times are simulated.
256 devices in a mesh: region: 32 (over z, x), cols: 8 (over y, core).
Axes of the slice: x: 4, y: 4, z: 8, core: 2. Of those that a mesh axis runs over, the one named last changes fastest.
Arguments:
- innovations: float32 [32, 262144], P('cols', 'region'), may hold values from -6 to 6
- coords: float32 [3, 262144], P(None, 'region'), may hold values from -1 to 1, as said below
- background_std: float32 [262144], P('region'), may hold values from 0.3 to 1.2
- obs_variance: float32 [262144], P('region'), may hold values from 0.25 to 1
- block_count: int32 [1024], P('region'), may hold values from 128 to 256, as said below
- pair_list: int32 [2, 24576], P(None, ('region', 'cols')), may hold values from 0 to 54, as said below
- pair_count: int32 [256], P(('region', 'cols')), may hold values from 4 to 96, as said below
Outputs:
- solution_field: float32 [32, 262144], P('cols', 'region')
- residual: float32 [32, 262144], P('cols', 'region')
Inputs may be any that keep to these rules, and one draw needn't show every extreme that they name: `coords`: every column is a unit vector. `block_count`: the first block of every region holds 256 live observations. `pair_list`: live entries of a device come first in its 96 slots; row 0 names a block whose index within the region lies among the device's own 32 // (devices on cols) blocks (the device at cols position c owns blocks c * that many onward), row 1 is at least row 0 and at most row 23, and the partner block exists; no unordered pair appears twice; dead slots hold 0. `pair_count`: some device has all 96 slots live.
All inputs are finite; a program needn't handle non-finite values.
Results may differ from a plain program's by a relative error of at most 0.0003.
Values sent between devices are 32-bit elements; how exact they have to be, the bound alone decides.
No kernel may reach another device: no remote copies, remote signals or barrier semaphores. Data moves between devices by JAX's collectives and lax.ppermute only.
A program may use at most 64 MiB of HBM per device.

v0:
```python
import jax
import jax.numpy as jnp
from jax import lax
from jax.sharding import PartitionSpec as P

BLOCK = 256
KMAX = 23
ITERS = 2


SUPPORT = 1000.0 / 6371.0
pair_group = 8


def from_behind(block, axis, distance):
    devices = range(lax.axis_size(axis))
    route = [(i - distance, i) for i in devices if i - distance in devices]
    return lax.ppermute(block, axis, route)


def cov_tiles(coord_blk, spread_blk, vec_blk, left_blocks, right_blocks, weights):
    left_pts = coord_blk[:, left_blocks]
    right_pts = coord_blk[:, right_blocks]
    inner_sum = left_pts[0][:, :, None] * right_pts[0][:, None, :]
    inner_sum = inner_sum + left_pts[1][:, :, None] * right_pts[1][:, None, :]
    inner_sum = inner_sum + left_pts[2][:, :, None] * right_pts[2][:, None, :]
    distance_ratio = jnp.sqrt(jnp.maximum(2.0 - 2.0 * inner_sum, 0.0)) / SUPPORT
    falloff = jnp.maximum(1.0 - distance_ratio, 0.0) ** 4 * (4.0 * distance_ratio + 1.0)
    tile_values = (
        spread_blk[left_blocks][:, :, None] * falloff * spread_blk[right_blocks][:, None, :]
    )
    into_left = jnp.einsum(
        "rgb,gab->rga", vec_blk[:, right_blocks], tile_values, precision=lax.Precision.HIGHEST
    )
    into_left = into_left * weights[None, :, None]
    mirror = weights * (left_blocks != right_blocks).astype(weights.dtype)
    into_right = jnp.einsum(
        "rga,gab->rgb", vec_blk[:, left_blocks], tile_values, precision=lax.Precision.HIGHEST
    )
    into_right = into_right * mirror[None, :, None]
    return (into_left, into_right)


def per_device(
    innovations, coords, background_std, obs_variance, block_count, pair_list, pair_count
):
    nblocks = block_count.shape[0]
    reach_blocks = KMAX
    live_mask = (jnp.arange(BLOCK)[None, :] < block_count[:, None]).astype(jnp.float32).reshape(-1)
    spread = background_std * live_mask
    next_coords, next_spread = from_behind((coords, spread), "region", -1)
    coord_blk = jnp.concatenate([coords, next_coords], 1).reshape(3, 2 * nblocks, BLOCK)
    spread_blk = jnp.concatenate([spread, next_spread], 0).reshape(2 * nblocks, BLOCK)
    turn_count = (pair_count[0] + pair_group - 1) // pair_group

    def pick_pairs(turn_index):
        left_blocks = lax.dynamic_slice_in_dim(pair_list[0], turn_index * pair_group, pair_group)
        right_blocks = lax.dynamic_slice_in_dim(pair_list[1], turn_index * pair_group, pair_group)
        weights = (turn_index * pair_group + jnp.arange(pair_group) < pair_count[0]).astype(
            jnp.float32
        )
        return (left_blocks, right_blocks, weights)

    reach_cells = reach_blocks * BLOCK
    own_cells = nblocks * BLOCK

    def squares(residual):
        return lax.psum(jnp.sum(residual * residual, axis=1), "region")

    solution_field = jnp.zeros_like(innovations)
    residual = innovations
    direction = innovations
    norm_now = squares(residual)
    for step_index in range(ITERS):
        all_columns = lax.all_gather(direction, "cols", axis=0, tiled=True)
        following = from_behind(all_columns[:, :reach_cells], "region", -1)
        row_total = all_columns.shape[0]
        extended = jnp.concatenate([all_columns, following], 1).reshape(
            row_total, nblocks + reach_blocks, BLOCK
        )
        vec_blk = extended

        def one_turn(turn_index, totals):
            left_blocks, right_blocks, weights = pick_pairs(turn_index)
            into_left, into_right = cov_tiles(
                coord_blk, spread_blk, vec_blk, left_blocks, right_blocks, weights
            )
            return totals.at[:, left_blocks].add(into_left).at[:, right_blocks].add(into_right)

        products = lax.fori_loop(0, turn_count, one_turn, jnp.zeros_like(vec_blk))
        own_part = products[:, :nblocks].reshape(row_total, -1)
        spill_part = products[:, nblocks:].reshape(row_total, -1)
        arriving = from_behind(spill_part, "region", 1)
        arriving = jnp.pad(arriving, ((0, 0), (0, own_cells - reach_cells)))
        summed = lax.psum_scatter(own_part + arriving, "cols", scatter_dimension=0, tiled=True)
        image = summed + obs_variance[None, :] * direction
        alpha = norm_now / lax.psum(jnp.sum(direction * image, axis=1), "region")
        solution_field = solution_field + alpha[:, None] * direction
        residual = residual - alpha[:, None] * image
        norm_next = squares(residual)
        direction = residual + (norm_next / norm_now)[:, None] * direction
        norm_now = norm_next
    return (solution_field, residual)


def solution(mesh):
    placed = (
        P("cols", "region"),
        P(None, "region"),
        P("region"),
        P("region"),
        P("region"),
        P(None, ("region", "cols")),
        P(("region", "cols")),
    )
    return jax.shard_map(
        per_device,
        mesh=mesh,
        in_specs=placed,
        out_specs=(P("cols", "region"), P("cols", "region")),
        check_vma=False,
    )
```

profile of v0, /device:TPU:2, one launch (start us, length us, event | category | flops | bytes accessed | tf_op | source)
XLA Modules:
  0.0 932.5 jit_solution(2691881738075963592)
XLA Ops:
  9.5 4.2 collective-permute-start
  16.3 22.5 %all-gather.5.cloned.1.call-done = f32[8,4,8192]{2,1,0:T(4,128)} async-done(((f32[1,4,8192]{2,1,0:T(4,128)}), f32[8,4,8192]{2,1,0:T(4,128)}) %all-gather.5.cloned.1.call-update) | async-done | bytes 1048592 | tf_op jit(solution)/shard_map/all_gather | solution.py:75
  40.4 2.5 collective-permute-start.2
  43.0 18.3 %collective-permute-done.2 = f32[32,5888]{1,0:T(8,128)S(1)} collective-permute-done((f32[32,5888]{1,0:T(8,128)S(1)}, f32[32,5888]{1,0:T(8,128)S(1)}, u32[]{:S(2)}, u32[]{:S(2)}) %collective-permute-start.2) | collective-permute-done | bytes 753696 | tf_op jit(solution)/shard_map/ppermute | solution.py:18
  63.6 130.2 %while.24 = (s32[]{:T(128)}, f32[32,55,256]{2,0,1:T(8,128)S(1)}, s32[]{:T(128)}, s32[2,96]{1,0:T(2,128)S(1)}, f32[64,256]{1,0:T(8,128)S(1)}, /*index=5*/f32[3,64...) while((s32[]{:T(128)}, f32[32,55,256]{2,0,1:T(8,128)S(1)}, ...), condition=%wide.region_5.6_spmd, body=%wide.region_2.5_spmd.sunk | while | flops 421793920 | bytes 4147635 | solution.py:90
  66.1 2.1 gather_fusion.4
  68.9 5.0 fusion.65
  74.8 2.1 gather_fusion.5
  76.8 4.4 fusion.66
  84.7 2.1 gather_fusion.4
  87.5 5.0 fusion.65
  93.4 2.1 gather_fusion.5
  95.4 4.4 fusion.66
  103.3 2.1 gather_fusion.4
  106.1 5.0 fusion.65
  112.0 2.1 gather_fusion.5
  114.1 4.4 fusion.66
  121.9 2.1 gather_fusion.4
  124.7 5.0 fusion.65
  130.6 2.1 gather_fusion.5
  132.7 4.4 fusion.66
  140.5 2.1 gather_fusion.4
  143.3 5.0 fusion.65
  149.2 2.1 gather_fusion.5
  151.3 4.4 fusion.66
  159.2 2.1 gather_fusion.4
  161.9 5.0 fusion.65
  167.8 2.1 gather_fusion.5
  169.9 4.4 fusion.66
  177.8 2.1 gather_fusion.4
  180.6 5.0 fusion.65
  186.4 2.1 gather_fusion.5
  188.5 4.4 fusion.66
  196.1 11.4 %collective-permute-done.3 = f32[32,5888]{1,0:T(8,128)S(1)} collective-permute-done((f32[32,5888]{1,0:T(8,128)S(1)}, f32[32,5888]{1,0:T(8,128)S(1)}, u32[]{:S(2)}, u32[]{:S(2)}) %collective-permute-start.3) | collective-permute-done | bytes 753696 | tf_op jit(solution)/shard_map/ppermute | solution.py:18
  209.9 150.0 %all-reduce.8.cloned.1.call-done = f32[32,8192]{1,0:T(8,128)} async-done(((f32[32,8192]{1,0:T(8,128)}), f32[32,8192]{1,0:T(8,128)}) %all-reduce.8.cloned.1.call-update) | async-done | bytes 1048592
  361.1 71.1 %all-reduce.4 = (f32[4]{0:T(128)S(1)}, f32[4]{0:T(128)S(1)}) all-reduce(f32[4]{0:T(128)S(1)} %get-tuple-element.245, f32[4]{0:T(128)S(1)} %get-tuple-element.244), channel_id=1, replica_groups=mesh['region'=32,'cols'=8] {'region'}, use_global_device_ids=true, to_apply=%region_1.2 | all-reduce | flops 8 | bytes 64 | tf_op jit(solution)/shard_map/psum | solution.py:68
  433.5 74.1 %psum.30 = f32[4]{0:T(128)S(1)} all-reduce(f32[4]{0:T(128)S(1)} %multiply_reduce_fusion.1), channel_id=1, replica_groups=mesh['region'=32,'cols'=8] {'region'}, use_global_device_ids=true, to_apply=%region_10.11 | all-reduce | flops 4 | bytes 32 | tf_op jit(solution)/shard_map/psum | solution.py:68
  509.4 20.5 %all-gather.7.cloned.1.call-done = f32[8,4,8192]{2,1,0:T(4,128)} async-done(((f32[1,4,8192]{2,1,0:T(4,128)}), f32[8,4,8192]{2,1,0:T(4,128)}) %all-gather.7.cloned.1.call-update) | async-done | bytes 1048592 | tf_op jit(solution)/shard_map/all_gather | solution.py:75
  532.4 2.5 collective-permute-start.4
  534.9 18.6 %collective-permute-done.4 = f32[32,5888]{1,0:T(8,128)S(1)} collective-permute-done((f32[32,5888]{1,0:T(8,128)}, f32[32,5888]{1,0:T(8,128)S(1)}, u32[]{:S(2)}, u32[]{:S(2)}) %collective-permute-start.4) | collective-permute-done | bytes 753696 | tf_op jit(solution)/shard_map/ppermute | solution.py:18
  555.4 130.2 %while.25 = (s32[]{:T(128)}, f32[32,55,256]{2,0,1:T(8,128)S(1)}, s32[]{:T(128)}, s32[2,96]{1,0:T(2,128)S(1)}, f32[64,256]{1,0:T(8,128)S(1)}, /*index=5*/f32[3,64...) while((s32[]{:T(128)}, f32[32,55,256]{2,0,1:T(8,128)S(1)}, ...), condition=%wide.region_14.15_spmd, body=%wide.region_11.14_spmd.sunk | while | flops 421793920 | bytes 4147635 | solution.py:90
  560.7 5.0 fusion.73
  568.6 4.4 fusion.74
  579.3 5.0 fusion.73
  587.2 4.4 fusion.74
  597.9 5.0 fusion.73
  605.8 4.4 fusion.74
  613.7 2.1 gather_fusion.10
  616.5 5.0 fusion.73
  622.4 2.1 gather_fusion.11
  624.4 4.4 fusion.74
  632.3 2.1 gather_fusion.10
  635.1 5.0 fusion.73
  641.0 2.1 gather_fusion.11
  643.0 4.4 fusion.74
  653.7 5.0 fusion.73
  659.6 2.1 gather_fusion.11
  661.6 4.4 fusion.74
  672.3 5.0 fusion.73
  678.2 2.1 gather_fusion.11
  680.2 4.4 fusion.74
  687.8 11.4 %collective-permute-done.5 = f32[32,5888]{1,0:T(8,128)S(1)} collective-permute-done((f32[32,5888]{1,0:T(8,128)S(1)}, f32[32,5888]{1,0:T(8,128)S(1)}, u32[]{:S(2)}, u32[]{:S(2)}) %collective-permute-start.5) | collective-permute-done | bytes 753696 | tf_op jit(solution)/shard_map/ppermute | solution.py:18
  700.3 151.3 %all-reduce.10.cloned.1.call-done = f32[32,8192]{1,0:T(8,128)} async-done(((f32[32,8192]{1,0:T(8,128)}), f32[32,8192]{1,0:T(8,128)}) %all-reduce.10.cloned.1.call-update) | async-done | bytes 1048592
  852.9 71.1 %psum.31 = f32[4]{0:T(128)S(1)} all-reduce(f32[4]{0:T(128)S(1)} %multiply_reduce_fusion), channel_id=1, replica_groups=mesh['region'=32,'cols'=8] {'region'}, use_global_device_ids=true, to_apply=%region_17.18 | all-reduce | flops 4 | bytes 32 | tf_op jit(solution)/shard_map/psum | solution.py:97
  (362 shorter events, 112.7 us)
Async XLA Ops:
  7.2 31.6 %all-gather.5.cloned.1.call-start = ((), (), s32[]{:S(2)}) async-start(), calls=%async_computation | async-start | bytes 1179648 | tf_op jit(solution)/shard_map/all_gather | solution.py:75
  7.9 352.1 %all-reduce.8.cloned.1.call-start = ((), (), s32[]{:S(2)}) async-start(), calls=%async_computation.2 | async-start | bytes 2097152
  9.5 6.8 collective-permute-start
  13.6 29.3 %collective-permute-start.1 = (f32[3,8192]{1,0:T(4,128)}, f32[3,8192]{1,0:T(4,128)S(1)}, u32[]{:S(2)}, u32[]{:S(2)}) collective-permute-start(f32[3,8192]{1,0:T(4,128)} %param.12), channel_id=1, source_target_pairs={{8,0},{16,8},{24,16},{32,24},{40,32},{48,40},{56,48},{64,56},{72,6... | collective-permute-start | bytes 294920 | tf_op jit(solution)/shard_map/ppermute | solution.py:18
  16.3 26.6 %copy-start.2 = (f32[3,8192]{1,0:T(4,128)S(1)}, f32[3,8192]{1,0:T(4,128)}, u32[]{:S(2)}) copy-start(f32[3,8192]{1,0:T(4,128)} %param.12) | copy-start | bytes 294916
  40.4 20.9 %collective-permute-start.2 = (f32[32,5888]{1,0:T(8,128)S(1)}, f32[32,5888]{1,0:T(8,128)S(1)}, u32[]{:S(2)}, u32[]{:S(2)}) collective-permute-start(f32[32,5888]{1,0:T(8,128)S(1)} %slice.156), channel_id=1, source_target_pairs={{8,0},{16,8},{24,16},{32,24},{40,32},{48,40},{56,48},{64,56},{72,6... | collective-permute-start | bytes 2261000 | tf_op jit(solution)/shard_map/ppermute | solution.py:18
  62.9 0.7 copy-start.3
  194.0 13.5 %collective-permute-start.3 = (f32[32,5888]{1,0:T(8,128)S(1)}, f32[32,5888]{1,0:T(8,128)S(1)}, u32[]{:S(2)}, u32[]{:S(2)}) collective-permute-start(f32[32,5888]{1,0:T(8,128)S(1)} %bitcast.196), channel_id=1, source_target_pairs={{0,8},{8,16},{16,24},{24,32},{32,40},{40,48},{48,56},{56,64},{64,7... | collective-permute-start | bytes 2261000 | tf_op jit(solution)/shard_map/ppermute | solution.py:18
  207.5 1.2 copy-start.4
  207.5 152.5 %copy-start = (f32[4,8192]{1,0:T(4,128)S(1)}, f32[4,8192]{1,0:T(4,128)}, u32[]{:S(2)}) copy-start(f32[4,8192]{1,0:T(4,128)} %param.11) | copy-start | bytes 393220
  207.5 152.5 %copy-start.1 = (f32[8192]{0:T(1024)S(1)}, f32[8192]{0:T(1024)}, u32[]{:S(2)}) copy-start(f32[8192]{0:T(1024)} %param.14) | copy-start | bytes 98308
  208.6 321.3 %all-gather.7.cloned.1.call-start = ((), (), s32[]{:S(2)}) async-start(), calls=%async_computation.1 | async-start | bytes 1179648 | tf_op jit(solution)/shard_map/all_gather | solution.py:75
  509.3 342.3 %all-reduce.10.cloned.1.call-start = ((), (), s32[]{:S(2)}) async-start(), calls=%async_computation.3 | async-start | bytes 2097152
  532.4 21.1 %collective-permute-start.4 = (f32[32,5888]{1,0:T(8,128)}, f32[32,5888]{1,0:T(8,128)S(1)}, u32[]{:S(2)}, u32[]{:S(2)}) collective-permute-start(f32[32,5888]{1,0:T(8,128)} %slice.157), channel_id=1, source_target_pairs={{8,0},{16,8},{24,16},{32,24},{40,32},{48,40},{56,48},{64,56},{72,6... | collective-permute-start | bytes 2261000 | tf_op jit(solution)/shard_map/ppermute | solution.py:18
  685.7 13.5 %collective-permute-start.5 = (f32[32,5888]{1,0:T(8,128)S(1)}, f32[32,5888]{1,0:T(8,128)S(1)}, u32[]{:S(2)}, u32[]{:S(2)}) collective-permute-start(f32[32,5888]{1,0:T(8,128)S(1)} %bitcast.197), channel_id=1, source_target_pairs={{0,8},{8,16},{16,24},{24,32},{32,40},{40,48},{48,56},{56,64},{64,7... | collective-permute-start | bytes 2261000 | tf_op jit(solution)/shard_map/ppermute | solution.py:18
Sparse Core Ops, SparseCore 0:
  9.9 28.8 all-gather.4
  208.8 151.1 all-reduce.7
  509.4 20.4 all-gather.6
  700.5 151.1 all-reduce.9
where the time goes:
time: 937 us; the launch traced here: 932 us
  waiting for transfers between devices  405 us (43%)
  blocking collectives  216 us (23%)
  matrix products  131 us (14%)
  local copies, waits for them, and re-layouts  99.3 us (11%)
  other arithmetic  47.8 us (5%)
  between operations  15.3 us (2%)
  starting transfers between devices  15 us (2%)
    unnamed x6, waiting for transfers between devices  302 us
    psum x2, blocking collectives, squares(): return lax.psum(jnp.sum(residual * residual, axis=1), 'region')  145 us
    psum x1, blocking collectives, per_device(): alpha = norm_now / lax.psum(jnp.sum(direction * image, axis=1), 'region')  71.1 us
    dot_general x14, matrix products, cov_tiles(): jnp.einsum('rgb,gab->rga', vec_blk[:, right_blocks], tile_values, precisi...  69.6 us
    dot_general x14, matrix products, cov_tiles(): jnp.einsum('rga,gab->rgb', vec_blk[:, left_blocks], tile_values, precisio...  61.8 us
    ppermute x6, waiting for transfers between devices, from_behind(): return lax.ppermute(block, axis, route)  59.8 us
    all_gather x2, waiting for transfers between devices, per_device(): all_columns = lax.all_gather(direction, 'cols', axis=0, tiled=True)  43 us
    gather x14, local copies, waits for them, and re-layouts, cov_tiles(): vec_blk[:, left_blocks]  28.7 us
  transfers between devices with their start and end apart: 10, of which 8 were waited for; matrix products, arithmetic and copies ran while one was open for 0% of the time, Pallas kernels for 0%

commit v1 on v0

v1 whole, which is shorter than its diff:
```python
import functools

import jax
import jax.numpy as jnp
from jax import lax
from jax.experimental import pallas as pl
from jax.experimental.pallas import tpu as pltpu
from jax.sharding import PartitionSpec as P

BLOCK = 256
KMAX = 23
SUPPORT = 1000.0 / 6371.0

STRETCH = 4.0**0.2
TOP = 5.0 / STRETCH**4
GAMMA = 2.0 * STRETCH**2 / SUPPORT**2
FAR = 2.0**100

ROWS = 32
CHIP = 8 * BLOCK
HALF = 4 * BLOCK
WIDE = CHIP + 128
AXES = ("region", "cols")

bf16 = jnp.bfloat16
f32 = jnp.float32


def dot(a, b):
    return jnp.dot(a, b, preferred_element_type=f32)


def two_parts(x):
    high = x.astype(bf16)
    return high, (x - high.astype(f32)).astype(bf16)


def three_parts(x):
    first = x.astype(bf16).astype(f32)
    rest = x - first
    second = rest.astype(bf16).astype(f32)
    return first, second, (rest - second).astype(bf16).astype(f32)


def vmem(count):
    return [pl.BlockSpec(memory_space=pltpu.VMEM)] * count


def smem(count):
    return [pl.BlockSpec(memory_space=pltpu.SMEM)] * count


def params(mebibytes):
    return pltpu.CompilerParams(vmem_limit_bytes=mebibytes * 1024 * 1024)


def prepare_kernel(
    place, counts, gathered, coords, std, variance, halo, vector, aux
):
    row_at, core = place[0], place[1]
    halo[32:40, :] = jnp.zeros((8, WIDE), f32)
    halo[0:32, CHIP:] = jnp.zeros((32, 128), f32)
    lane = lax.broadcasted_iota(jnp.int32, (1, BLOCK), 1)
    for j in range(8):
        source = j + core * (7 - 2 * j)
        here = slice(j * BLOCK, (j + 1) * BLOCK)
        local = pl.ds(pl.multiple_of(source * BLOCK, BLOCK), BLOCK)
        region = pl.ds(pl.multiple_of((row_at * 8 + source) * BLOCK, BLOCK), BLOCK)
        live = (lane < counts[row_at * 8 + source]).astype(f32)
        spread = std[0:1, region] * live
        values = gathered[:, local]
        vector[:, here] = values
        halo[0:32, here] = values * spread
        halo[32:35, here] = coords[:, region]
        aux[0:1, here] = spread
        aux[1:2, here] = variance[0:1, region]
    sub = lax.broadcasted_iota(jnp.int32, (8, 128), 0)
    col = lax.broadcasted_iota(jnp.int32, (8, 128), 1)
    far = col < 24
    mine = col - lax.div(col, 8) * 8
    ahead = 8 * (lax.div(col, 8) + 1)
    offset = jnp.where(far, ahead + sub - mine, jnp.abs(mine - sub))
    left_up = jnp.where(far, mine, jnp.minimum(mine, sub))
    left_down = jnp.where(far, 7 - sub, 7 - jnp.maximum(mine, sub))
    left = jnp.where(core == 0, left_up, left_down)
    valid = (offset >= 0) & (offset <= KMAX) & (col < 32)
    target = jnp.where(valid, (row_at * 8 + left) * 24 + offset, -7).astype(f32)
    codes = gathered[pl.ds(pl.multiple_of(row_at * 8, 8), 8), CHIP:WIDE]
    hit = jnp.zeros((8, 128), f32)
    for source in (0, 4):
        for i in range(96):
            code = jnp.broadcast_to(codes[source : source + 1, i : i + 1], (8, 128))
            hit = jnp.where(code == target, 1.0, hit)
    halo[32:40, CHIP:] = jnp.where(hit > 0.5, 0.0, FAR)


def prepare(place, counts, gathered, coords, std, variance):
    return pl.pallas_call(
        prepare_kernel,
        out_shape=(
            jax.ShapeDtypeStruct((40, WIDE), f32),
            jax.ShapeDtypeStruct((ROWS, CHIP), f32),
            jax.ShapeDtypeStruct((8, CHIP), f32),
        ),
        in_specs=smem(2) + vmem(4),
        out_specs=vmem(3),
        compiler_params=params(8),
        name="prepare",
    )(place, counts, gathered, coords, std, variance)


def covariance(left, right):
    x = jnp.maximum(dot(left, right), 1e-30)
    z = jnp.maximum(STRETCH - x * lax.rsqrt(x), 0.0)
    z2 = z * z
    return two_parts(z2 * z2 * (TOP - z))


def own_side(own):
    sub = lax.broadcasted_iota(jnp.int32, (8, CHIP), 0)
    points = own[32:40, 0:CHIP]
    side = jnp.where(sub < 3, points * (-GAMMA), jnp.where(sub == 3, GAMMA, 0.0))
    return three_parts(side)


def far_side(points):
    sub = lax.broadcasted_iota(jnp.int32, (8, BLOCK), 0)
    b1, b2, b3 = three_parts(
        jnp.where(sub < 3, points, jnp.where(sub < 5, 1.0, 0.0))
    )
    return jnp.concatenate([b1, b2, b1, b2, b3, b1], 0).T.astype(bf16)


def masks(place, own, halo, offset, spread_out):
    column = 24 if offset == 0 else 8 * (offset - 1)
    flags = jnp.where(
        place[1] == 0, own[32:40, CHIP:WIDE], halo[32:40, CHIP:WIDE]
    )
    for a in range(8):
        spread_out[:, a * BLOCK : (a + 1) * BLOCK] = jnp.broadcast_to(
            flags[:, column + a : column + a + 1], (8, BLOCK)
        )


def tiles_kernel(offset, place, own, halo, before, high, low, total, right, mask):
    a1, a2, a3 = own_side(own)
    right[16:32, :] = jnp.concatenate([a2, a2], 0).astype(bf16)
    right[32:48, :] = jnp.concatenate([a1, a3], 0).astype(bf16)
    masks(place, own, halo, offset, mask)
    if offset == 0:
        total[...] = jnp.zeros_like(total)
    else:
        total[...] = before[...]
    sub = lax.broadcasted_iota(jnp.int32, (8, CHIP), 0)

    def one_block(b, carry):
        rows = pl.ds(pl.multiple_of(b * BLOCK, BLOCK), BLOCK)
        left = far_side(halo[32:40, rows])
        row = jnp.broadcast_to(mask[pl.ds(b, 1), :], (8, CHIP))
        right[0:16, :] = jnp.concatenate(
            [jnp.where(sub == 4, row, a1), a1], 0
        ).astype(bf16)
        uh, ul = two_parts(halo[0:32, rows])
        both = jnp.concatenate([uh, ul], 0)
        for a in range(8):
            here = slice(a * BLOCK, (a + 1) * BLOCK)
            th, tl = covariance(left, right[:, here])
            high[rows, here] = th
            low[rows, here] = tl
            total[:, here] += dot(both, th)
            total[0:32, here] += dot(uh, tl)
        return carry

    lax.fori_loop(0, 4 if offset == 0 else 8, one_block, 0)


def tiles(offset, place, own, halo, before):
    depth = HALF if offset == 0 else CHIP
    return pl.pallas_call(
        functools.partial(tiles_kernel, offset),
        out_shape=(
            pltpu.VMEM((depth, CHIP), bf16),
            pltpu.VMEM((depth, CHIP), bf16),
            jax.ShapeDtypeStruct((2 * ROWS, CHIP), f32),
        ),
        in_specs=smem(1) + vmem(3),
        out_specs=vmem(3),
        scratch_shapes=[pltpu.VMEM((48, CHIP), bf16), pltpu.VMEM((8, CHIP), f32)],
        compiler_params=params(10),
        name=f"tiles{offset}",
    )(place, own, halo, before)


def edge_kernel(place, own, halo, before, high, low, product, right, first, mask, left, total):
    a1, a2, a3 = own_side(own)
    right[0:16, :] = jnp.concatenate([a2, a2], 0).astype(bf16)
    right[16:32, :] = jnp.concatenate([a1, a3], 0).astype(bf16)
    masks(place, own, halo, 3, mask)
    total[...] = before[...]
    sub = lax.broadcasted_iota(jnp.int32, (8, CHIP), 0)

    def one_side(j, carry):
        rows = pl.ds(pl.multiple_of(j * BLOCK, BLOCK), BLOCK)
        left[rows, :] = far_side(halo[32:40, rows])
        row = jnp.broadcast_to(mask[pl.ds(j, 1), :], (8, CHIP))
        first[pl.ds(pl.multiple_of(j * 16, 16), 16), :] = jnp.concatenate(
            [jnp.where(sub == 4, row, a1), a1], 0
        ).astype(bf16)
        return carry

    lax.fori_loop(0, 7, one_side, 0)

    def one_group(g, carry):
        for s in range(7):
            inner = s < 7 - g
            j = jnp.where(inner, g, 7 - g)
            a = s + 1 + jnp.where(inner, g, 0)
            rows = pl.ds(pl.multiple_of(j * BLOCK, BLOCK), BLOCK)
            here = pl.ds(pl.multiple_of(a * BLOCK, BLOCK), BLOCK)
            at = (lax.div(a * (a - 1), 2) + j) * BLOCK
            keep = pl.ds(pl.multiple_of(at, BLOCK), BLOCK)
            side = jnp.concatenate(
                [
                    first[pl.ds(pl.multiple_of(j * 16, 16), 16), here],
                    right[:, here],
                ],
                0,
            )
            th, tl = covariance(left[rows, :], side)
            high[keep, :] = th
            low[keep, :] = tl
            uh, ul = two_parts(halo[0:32, rows])
            total[:, here] += dot(jnp.concatenate([uh, ul], 0), th)
            total[0:32, here] += dot(uh, tl)
        return carry

    lax.fori_loop(0, 4, one_group, 0)
    product[...] = total[0:32, :] + total[32:64, :]


def edge_tiles(place, own, halo, before):
    return pl.pallas_call(
        edge_kernel,
        out_shape=(
            pltpu.VMEM((28 * BLOCK, BLOCK), bf16),
            pltpu.VMEM((28 * BLOCK, BLOCK), bf16),
            jax.ShapeDtypeStruct((ROWS, CHIP), f32),
        ),
        in_specs=smem(1) + vmem(3),
        out_specs=vmem(3),
        scratch_shapes=[
            pltpu.VMEM((32, CHIP), bf16),
            pltpu.VMEM((7 * 16, CHIP), bf16),
            pltpu.VMEM((8, CHIP), f32),
            pltpu.VMEM((CHIP, 48), bf16),
            pltpu.VMEM((2 * ROWS, CHIP), f32),
        ],
        compiler_params=params(10),
        name="tiles3",
    )(place, own, halo, before)


def apply_kernel(depth, vector, high, low, before, total):
    uh, ul = two_parts(vector[:, 0:depth])
    both = jnp.concatenate([uh, ul], 0)
    for n in range(0, CHIP, 512):
        here = slice(n, n + 512)
        pair = dot(both, high[:, here])
        extra = dot(uh, low[:, here])
        total[:, here] = before[:, here] + ((pair[0:32] + pair[32:64]) + extra)


def apply(vector, high, low, before):
    depth = high.shape[0]
    return pl.pallas_call(
        functools.partial(apply_kernel, depth),
        out_shape=jax.ShapeDtypeStruct((ROWS, CHIP), f32),
        in_specs=vmem(4),
        out_specs=vmem(1)[0],
        compiler_params=params(8),
        name="apply",
    )(vector, high, low, before)


def edge_apply_kernel(vector, high, low, before, total):
    uh, ul = two_parts(vector[...])
    both = jnp.concatenate([uh, ul], 0)
    total[:, 0:BLOCK] = before[:, 0:BLOCK]
    for a in range(1, 8):
        rows = slice(a * (a - 1) // 2 * BLOCK, a * (a + 1) // 2 * BLOCK)
        here = slice(a * BLOCK, (a + 1) * BLOCK)
        pair = dot(both[:, 0 : a * BLOCK], high[rows, :])
        extra = dot(uh[:, 0 : a * BLOCK], low[rows, :])
        total[:, here] = before[:, here] + ((pair[0:32] + pair[32:64]) + extra)


def edge_apply(vector, high, low, before):
    return pl.pallas_call(
        edge_apply_kernel,
        out_shape=jax.ShapeDtypeStruct((ROWS, CHIP), f32),
        in_specs=vmem(4),
        out_specs=vmem(1)[0],
        compiler_params=params(8),
        name="apply3",
    )(vector, high, low, before)


def combine_kernel(mine, other, aux, vector, image, scaled):
    for j in range(8):
        here = slice(j * BLOCK, (j + 1) * BLOCK)
        there = slice((7 - j) * BLOCK, (8 - j) * BLOCK)
        spread = aux[0:1, here]
        value = (mine[:, here] + other[:, there]) * spread
        value = value + aux[1:2, here] * vector[:, here]
        image[:, here] = value
        scaled[:, here] = value * spread


def combine(mine, other, aux, vector):
    shape = jax.ShapeDtypeStruct((ROWS, CHIP), f32)
    return pl.pallas_call(
        combine_kernel,
        out_shape=(shape, shape),
        in_specs=vmem(4),
        out_specs=vmem(2),
        compiler_params=params(8),
        name="combine",
    )(mine, other, aux, vector)


def finish_kernel(place, mine, other, aux, vector, image, out):
    core = place[1]
    sums = [jnp.zeros((ROWS, 1), f32) for _ in range(4)]
    for j in range(4):
        here = slice(j * BLOCK, (j + 1) * BLOCK)
        there = slice((7 - j) * BLOCK, (8 - j) * BLOCK)
        last = (mine[:, here] + other[:, there]) * aux[0:1, here]
        last = last + aux[1:2, here] * image[:, here]
        place_at = j + core * (3 - 2 * j)
        out[:, pl.ds(pl.multiple_of(place_at * BLOCK, BLOCK), BLOCK)] = image[:, here]
        out[:, pl.ds(pl.multiple_of(HALF + place_at * BLOCK, BLOCK), BLOCK)] = last
        terms = (
            vector[:, here] * vector[:, here],
            vector[:, here] * image[:, here],
            image[:, here] * image[:, here],
            image[:, here] * last,
        )
        sums = [s + jnp.sum(t, axis=1, keepdims=True) for s, t in zip(sums, terms)]
    lane = lax.broadcasted_iota(jnp.int32, (ROWS, 128), 1)
    packed = jnp.zeros((ROWS, 128), f32)
    for i in range(4):
        packed = jnp.where(lane == i, sums[i], packed)
    out[:, CHIP:] = packed


def finish(place, mine, other, aux, vector, image):
    return pl.pallas_call(
        finish_kernel,
        out_shape=jax.ShapeDtypeStruct((ROWS, WIDE), f32),
        in_specs=smem(1) + vmem(5),
        out_specs=vmem(1)[0],
        compiler_params=params(8),
        name="finish",
    )(place, mine, other, aux, vector, image)


def neighbours(block, step, chips):
    route = [(2 * (m + step), 2 * m) for m in range(chips - step)]
    route += [(2 * m + 1, 2 * (m + step) + 1) for m in range(chips - step)]
    return lax.ppermute(block, AXES, route)


def sibling(block, chips):
    route = [(i, i ^ 1) for i in range(2 * chips)]
    return lax.ppermute(block, AXES, route)


def per_device(
    innovations, coords, background_std, obs_variance, block_count, pair_list, pair_count
):
    chips = lax.axis_size("region") * lax.axis_size("cols") // 2
    column = lax.axis_index("cols")
    place = jnp.stack([column // 2, column % 2]).astype(jnp.int32)

    slots = jnp.arange(128)
    codes = jnp.pad(pair_list[0] * 24 + (pair_list[1] - pair_list[0]), (0, 32))
    codes = jnp.where(slots < pair_count[0], codes, -1).astype(f32)
    rows = innovations.reshape(4, 4, CHIP).transpose(1, 0, 2)
    rows = jnp.concatenate([rows, jnp.broadcast_to(codes, (4, 4, 128))], 2)
    rows = jnp.broadcast_to(rows[:, None], (4, 2, 4, WIDE)).reshape(8, 4, WIDE)
    gathered = lax.all_to_all(rows, "cols", 0, 0, tiled=True).reshape(ROWS, WIDE)

    own, vector, aux = prepare(
        place,
        block_count,
        gathered,
        coords,
        background_std.reshape(1, -1),
        obs_variance.reshape(1, -1),
    )
    halos = [own] + [neighbours(own, step, chips) for step in (1, 2, 3)]
    kept, total = [], jnp.zeros((2 * ROWS, CHIP), f32)
    for offset in range(3):
        high, low, total = tiles(offset, place, own, halos[offset], total)
        kept.append((high, low))
    high, low, product = edge_tiles(place, own, halos[3], total)
    kept.append((high, low))
    image, scaled = combine(product, sibling(product, chips), aux, vector)

    halos = [scaled] + [neighbours(scaled, step, chips) for step in (1, 2, 3)]
    product = jnp.zeros((ROWS, CHIP), f32)
    for offset in range(3):
        product = apply(halos[offset], *kept[offset], product)
    product = edge_apply(halos[3], *kept[3], product)
    sent = finish(place, product, sibling(product, chips), aux, vector, image)

    back = lax.all_to_all(sent.reshape(8, 4, WIDE), "cols", 0, 0, tiled=True)
    first = back[:, :, 0:HALF].transpose(1, 0, 2).reshape(4, -1)
    second = back[:, :, HALF:CHIP].transpose(1, 0, 2).reshape(4, -1)
    sums = jnp.sum(back[:, :, CHIP : CHIP + 4], axis=0)
    regions = lax.axis_size("region")
    sums = lax.all_to_all(
        jnp.broadcast_to(sums.reshape(1, 16), (regions, 16)), "region", 0, 0, tiled=True
    )
    sums = jnp.sum(sums, axis=0).reshape(4, 4)
    bb, bk, kk, kl = (sums[:, i : i + 1] for i in range(4))
    alpha = bb / bk
    norm = alpha * alpha * kk - 2.0 * alpha * bk + bb
    beta = norm / bb
    grown = 1.0 + beta
    energy = grown * grown * bk - 2.0 * alpha * grown * kk + alpha * alpha * kl
    step = norm / energy
    direction = grown * innovations - alpha * first
    field = alpha * innovations + step * direction
    residual = innovations - alpha * first - step * (grown * first - alpha * second)
    return field, residual


def solution(mesh):
    placed = (
        P("cols", "region"),
        P(None, "region"),
        P("region"),
        P("region"),
        P("region"),
        P(None, ("region", "cols")),
        P(("region", "cols")),
    )
    return jax.shard_map(
        per_device,
        mesh=mesh,
        in_specs=placed,
        out_specs=(P("cols", "region"), P("cols", "region")),
        check_vma=False,
    )
```

time: 937 us -> 129 us (0.14)
  waiting for transfers between devices: 405 us -> 23.1 us
  blocking collectives: 216 us -> 11.4 us
  matrix products: 131 us -> 0 us
  local copies, waits for them, and re-layouts: 99.3 us -> 10.1 us
  Pallas kernels: 0 us -> 46.1 us
  other arithmetic: 47.8 us -> 2.14 us
  starting transfers between devices: 15 us -> 33.6 us
  between operations: 15.3 us -> 1.54 us
    unnamed x6 -> x0, waiting for transfers between devices: 302 us -> none
    psum x3 -> x0, blocking collectives: 216 us -> none  [the longest x2 145 us: squares(): return lax.psum(jnp.sum(residual * residual, axis=1), 'region')]
    dot_general x28 -> x0, matrix products: 131 us -> none  [the longest x14 69.6 us: cov_tiles(): jnp.einsum('rgb,gab->rga', vec_blk[:, right_blocks], tile_values, precisi...]
    gather x84 -> x0, local copies, waits for them, and re-layouts: 89.3 us -> none  [the longest x14 28.7 us: cov_tiles(): vec_blk[:, left_blocks]]
    ppermute x6 -> x8, waiting for transfers between devices: 59.8 us -> 7.03 us  [the longest x6 3.98 us: neighbours(): return lax.ppermute(block, AXES, route)]
    pallas_call x0 -> x11, Pallas kernels: none -> 46.1 us  [the longest x3 29.4 us: tiles(): pl.pallas_call(functools.partial(tiles_kernel, offset), out_shape=(pltpu....]
    all_gather x2 -> x0, waiting for transfers between devices: 43 us -> none  [per_device(): all_columns = lax.all_gather(direction, 'cols', axis=0, tiled=True)]
    scatter-add x28 -> x0, other arithmetic: 24.9 us -> none  [one_turn(): totals.at[:, left_blocks].add(into_left).at[:, right_blocks].add(into_right)]
  transfers between devices with their start and end apart: 10 -> 10, of which waited for: 8 -> 6; matrix products, arithmetic and copies ran while one was open for 0% -> 0% of each run, Pallas kernels for 0% -> 29%
where the time goes in v1:
time: 129 us; the launch traced here: 128 us
  Pallas kernels  46.1 us (36%)
  starting transfers between devices  33.6 us (26%)
  waiting for transfers between devices  23.1 us (18%)
  blocking collectives  11.4 us (9%)
  local copies, waits for them, and re-layouts  10.1 us (8%)
  other arithmetic  2.14 us (2%)
  between operations  1.54 us (1%)
    pallas_call x3, Pallas kernels, tiles(): pl.pallas_call(functools.partial(tiles_kernel, offset), out_shape=(pltpu....  29.4 us
    ppermute x6, starting transfers between devices, neighbours(): return lax.ppermute(block, AXES, route)  17.1 us
    all_to_all x1, starting transfers between devices, per_device(): lax.all_to_all(jnp.broadcast_to(sums.reshape(1, 16), (regions, 16)), 'reg...  11.9 us
    all_to_all x1, blocking collectives, per_device(): back = lax.all_to_all(sent.reshape(8, 4, WIDE), 'cols', 0, 0, tiled=True)  11.4 us
    all_to_all x1, waiting for transfers between devices, per_device(): lax.all_to_all(jnp.broadcast_to(sums.reshape(1, 16), (regions, 16)), 'reg...  8.42 us
    all_to_all x1, waiting for transfers between devices, per_device(): lax.all_to_all(rows, 'cols', 0, 0, tiled=True).reshape(ROWS, WIDE)  7.64 us
    pallas_call x3, Pallas kernels, apply(): pl.pallas_call(functools.partial(apply_kernel, depth), out_shape=jax.Shap...  7.53 us
    unnamed x14, local copies, waits for them, and re-layouts  7.21 us
  transfers between devices with their start and end apart: 10, of which 6 were waited for; matrix products, arithmetic and copies ran while one was open for 0% of the time, Pallas kernels for 29%

profile of v1, /device:TPU:2, one launch (start us, length us, event | category | flops | bytes accessed | tf_op | source)
XLA Modules:
  0.0 127.9 jit_solution(15469698583044314180)
XLA Ops:
  0.6 1.0 reshape.45
  1.7 0.8 add_bitcast_fusion
  3.2 0.7 broadcast_in_dim.28
  3.9 4.5 %all-to-all-start = ((f32[8,4,2176]{2,1,0:T(4,128)}), f32[8,4,2176]{2,1,0:T(4,128)S(1)}, u32[]{:S(2)}, u32[]{:S(2)}) async-start(f32[8,4,2176]{2,1,0:T(4,128)} %bitcast.5), calls=%async_computation | async-start | bytes 557056 | tf_op jit(solution)/shard_map/all_to_all | solution.py:391
  8.4 0.1 pad_add_fusion.place
  8.5 7.6 %all-to-all-done = f32[8,4,2176]{2,1,0:T(4,128)S(1)} async-done(((f32[8,4,2176]{2,1,0:T(4,128)}), f32[8,4,2176]{2,1,0:T(4,128)S(1)}, u32[]{:S(2)}, u32[]{:S(2)}) %all-to-all-start) | async-done | bytes 278560 | tf_op jit(solution)/shard_map/all_to_all | solution.py:391
  16.1 0.1 reshape.47.gathered
  16.2 0.0 copy-start.2
  16.2 0.9 copy-done.2
  17.1 0.0 copy-start.3
  17.1 0.8 copy-done.3
  17.9 0.0 copy-start.4
  17.9 0.8 copy-done.4
  18.6 0.0 copy-start.5
  18.6 0.7 copy-done.5
  19.3 0.9 prepare.1
  20.2 3.6 %collective-permute-start.2 = (f32[40,2176]{1,0:T(8,128)S(1)}, f32[40,2176]{1,0:T(8,128)S(1)}, u32[]{:S(2)}, u32[]{:S(2)}) collective-permute-start(f32[40,2176]{1,0:T(8,128)S(1)} %get-tuple-element.19.own.halo), channel_id=1, source_target_pairs={{2,0},{4,2},{6,4},{8,6},{10,8},{12,10},{14,12},{16,14},{18,16},{20... | collective-permute-start | bytes 1044488 | tf_op jit(solution)/shard_map/ppermute | solution.py:370
  23.9 3.4 %collective-permute-start.1 = (f32[40,2176]{1,0:T(8,128)S(1)}, f32[40,2176]{1,0:T(8,128)S(1)}, u32[]{:S(2)}, u32[]{:S(2)}) collective-permute-start(f32[40,2176]{1,0:T(8,128)S(1)} %get-tuple-element.19.own.halo), channel_id=1, source_target_pairs={{4,0},{6,2},{8,4},{10,6},{12,8},{14,10},{16,12},{18,14},{20,16},{2... | collective-permute-start | bytes 1044488 | tf_op jit(solution)/shard_map/ppermute | solution.py:370
  27.3 1.9 %collective-permute-start = (f32[40,2176]{1,0:T(8,128)S(1)}, f32[40,2176]{1,0:T(8,128)S(1)}, u32[]{:S(2)}, u32[]{:S(2)}) collective-permute-start(f32[40,2176]{1,0:T(8,128)S(1)} %get-tuple-element.19.own.halo), channel_id=1, source_target_pairs={{6,0},{8,2},{10,4},{12,6},{14,8},{16,10},{18,12},{20,14},{22,16},{... | collective-permute-start | bytes 1044488 | tf_op jit(solution)/shard_map/ppermute | solution.py:370
  29.2 6.1 %tiles0.1 = (bf16[1024,2048]{1,0:T(8,128)(2,1)S(1)}, bf16[1024,2048]{1,0:T(8,128)(2,1)S(1)}, f32[64,2048]{1,0:T(8,128)S(1)}) custom-call(s32[2]{0:T(128)S(1)} %pad_add_fusion.place, f32[40,2176]{1,0:T(8,128)S(1)} %get-tuple-element.19.own.halo, f32[40,2176]{1,0:T(8,128)S(1)} %get-tuple-element.19.own.halo, f32[64,2048]{1,0:T(8,128)S(1)} %broadcast_in_dim.29.before), custom_call_target="tpu_custom_call" | custom-call | tf_op jit(solution)/shard_map/tiles0/pallas_call | solution.py:179
  35.4 0.0 copy-start
  35.4 1.9 %copy-done = bf16[1024,2048]{1,0:T(8,128)(2,1)} copy-done((bf16[1024,2048]{1,0:T(8,128)(2,1)}, bf16[1024,2048]{1,0:T(8,128)(2,1)S(1)}, u32[]{:S(2)}) %copy-start) | copy-done | bytes 4194328
  37.3 0.8 collective-permute-done.2.halo
  38.1 11.7 %tiles1.1 = (bf16[2048,2048]{1,0:T(8,128)(2,1)S(1)}, bf16[2048,2048]{1,0:T(8,128)(2,1)S(1)}, f32[64,2048]{1,0:T(8,128)S(1)}) custom-call(s32[2]{0:T(128)S(1)} %pad_add_fusion.place, f32[40,2176]{1,0:T(8,128)S(1)} %get-tuple-element.19.own.halo, f32[40,2176]{1,0:T(8,128)S(1)} %collective-permute-done.2.halo, f32[64,2048]{1,0:T(8,128)S(1)} %get-tuple-element.20.before), custom_call_target="tpu_custom_call" | custom-call | tf_op jit(solution)/shard_map/tiles1/pallas_call | solution.py:179
  49.8 0.0 collective-permute-done.1.halo
  49.8 11.6 %tiles2.1 = (bf16[2048,2048]{1,0:T(8,128)(2,1)S(1)}, bf16[2048,2048]{1,0:T(8,128)(2,1)S(1)}, f32[64,2048]{1,0:T(8,128)S(1)}) custom-call(s32[2]{0:T(128)S(1)} %pad_add_fusion.place, f32[40,2176]{1,0:T(8,128)S(1)} %get-tuple-element.19.own.halo, f32[40,2176]{1,0:T(8,128)S(1)} %collective-permute-done.1.halo, f32[64,2048]{1,0:T(8,128)S(1)} %get-tuple-element.21.before), custom_call_target="tpu_custom_call" | custom-call | tf_op jit(solution)/shard_map/tiles2/pallas_call | solution.py:179
  61.4 0.0 collective-permute-done.halo
  61.5 6.2 %tiles3.1 = (bf16[7168,256]{1,0:T(8,128)(2,1)S(1)}, bf16[7168,256]{1,0:T(8,128)(2,1)S(1)}, f32[32,2048]{1,0:T(8,128)S(1)}) custom-call(s32[2]{0:T(128)S(1)} %pad_add_fusion.place, f32[40,2176]{1,0:T(8,128)S(1)} %get-tuple-element.19.own.halo, f32[40,2176]{1,0:T(8,128)S(1)} %collective-permute-done.halo, f32[64,2048]{1,0:T(8,128)S(1)} %get-tuple-element.22.before), custom_call_target="tpu_custom_call" | custom-call | tf_op jit(solution)/shard_map/tiles3/pallas_call | solution.py:242
  67.6 0.1 collective-permute-start.3
  67.7 1.5 %collective-permute-done.3.other = f32[32,2048]{1,0:T(8,128)S(1)} collective-permute-done((f32[32,2048]{1,0:T(8,128)S(1)}, f32[32,2048]{1,0:T(8,128)S(1)}, u32[]{:S(2)}, u32[]{:S(2)}) %collective-permute-start.3) | collective-permute-done | bytes 262176 | tf_op jit(solution)/shard_map/ppermute | solution.py:375
  69.2 0.1 combine.1
  69.3 3.2 %collective-permute-start.6 = (f32[32,2048]{1,0:T(8,128)S(1)}, f32[32,2048]{1,0:T(8,128)S(1)}, u32[]{:S(2)}, u32[]{:S(2)}) collective-permute-start(f32[32,2048]{1,0:T(8,128)S(1)} %get-tuple-element.26.vector), channel_id=1, source_target_pairs={{2,0},{4,2},{6,4},{8,6},{10,8},{12,10},{14,12},{16,14},{18,16},{20... | collective-permute-start | bytes 786440 | tf_op jit(solution)/shard_map/ppermute | solution.py:370
  72.5 2.9 %collective-permute-start.5 = (f32[32,2048]{1,0:T(8,128)S(1)}, f32[32,2048]{1,0:T(8,128)S(1)}, u32[]{:S(2)}, u32[]{:S(2)}) collective-permute-start(f32[32,2048]{1,0:T(8,128)S(1)} %get-tuple-element.26.vector), channel_id=1, source_target_pairs={{4,0},{6,2},{8,4},{10,6},{12,8},{14,10},{16,12},{18,14},{20,16},{2... | collective-permute-start | bytes 786440 | tf_op jit(solution)/shard_map/ppermute | solution.py:370
  75.4 2.1 %collective-permute-start.4 = (f32[32,2048]{1,0:T(8,128)S(1)}, f32[32,2048]{1,0:T(8,128)S(1)}, u32[]{:S(2)}, u32[]{:S(2)}) collective-permute-start(f32[32,2048]{1,0:T(8,128)S(1)} %get-tuple-element.26.vector), channel_id=1, source_target_pairs={{6,0},{8,2},{10,4},{12,6},{14,8},{16,10},{18,12},{20,14},{22,16},{... | collective-permute-start | bytes 786440 | tf_op jit(solution)/shard_map/ppermute | solution.py:370
  77.5 0.0 copy-start.1
  77.5 2.2 %copy-done.1 = bf16[1024,2048]{1,0:T(8,128)(2,1)S(1)} copy-done((bf16[1024,2048]{1,0:T(8,128)(2,1)S(1)}, bf16[1024,2048]{1,0:T(8,128)(2,1)}, u32[]{:S(2)}) %copy-start.1) | copy-done | bytes 4194328
  79.7 1.5 %apply.3.before = f32[32,2048]{1,0:T(8,128)S(1)} custom-call(f32[32,2048]{1,0:T(8,128)S(1)} %get-tuple-element.26.vector, bf16[1024,2048]{1,0:T(8,128)(2,1)S(1)} %get-tuple-element.33.high, bf16[1024,2048]{1,0:T(8,128)(2,1)S(1)} %copy-done.1, f32[32,2048]{1,0:T(8,128)S(1)} %broadcast_in_dim.30.before), custom_call_target="tpu_custom_call" | custom-call | tf_op jit(solution)/shard_map/apply/pallas_call | solution.py:275
  81.2 0.0 collective-permute-done.6.vector
  81.2 3.0 %apply.4.before = f32[32,2048]{1,0:T(8,128)S(1)} custom-call(f32[32,2048]{1,0:T(8,128)S(1)} %collective-permute-done.6.vector, bf16[2048,2048]{1,0:T(8,128)(2,1)S(1)} %get-tuple-element.31.high, bf16[2048,2048]{1,0:T(8,128)(2,1)S(1)} %get-tuple-element.32.low, f32[32,2048]{1,0:T(8,128)S(1)} %apply.3.before), custom_call_target="tpu_custom_call" | custom-call | tf_op jit(solution)/shard_map/apply/pallas_call | solution.py:275
  84.2 3.2 %collective-permute-done.5.vector = f32[32,2048]{1,0:T(8,128)S(1)} collective-permute-done((f32[32,2048]{1,0:T(8,128)S(1)}, f32[32,2048]{1,0:T(8,128)S(1)}, u32[]{:S(2)}, u32[]{:S(2)}) %collective-permute-start.5) | collective-permute-done | bytes 262176 | tf_op jit(solution)/shard_map/ppermute | solution.py:370
  87.4 3.0 %apply.5.before = f32[32,2048]{1,0:T(8,128)S(1)} custom-call(f32[32,2048]{1,0:T(8,128)S(1)} %collective-permute-done.5.vector, bf16[2048,2048]{1,0:T(8,128)(2,1)S(1)} %get-tuple-element.29.high, bf16[2048,2048]{1,0:T(8,128)(2,1)S(1)} %get-tuple-element.30.low, f32[32,2048]{1,0:T(8,128)S(1)} %apply.4.before), custom_call_target="tpu_custom_call" | custom-call | tf_op jit(solution)/shard_map/apply/pallas_call | solution.py:275
  90.4 0.0 copy-start.6
  90.4 0.0 collective-permute-done.4.vector
  90.4 1.3 %apply3.1.mine = f32[32,2048]{1,0:T(8,128)S(1)} custom-call(f32[32,2048]{1,0:T(8,128)S(1)} %collective-permute-done.4.vector, bf16[7168,256]{1,0:T(8,128)(2,1)S(1)} %get-tuple-element.27.high, bf16[7168,256]{1,0:T(8,128)(2,1)S(1)} %get-tuple-element.28.low, f32[32,2048]{1,0:T(8,128)S(1)} %apply.5.before), custom_call_target="tpu_custom_call" | custom-call | tf_op jit(solution)/shard_map/apply3/pallas_call | solution.py:298
  91.7 0.0 collective-permute-start.7
  91.8 1.5 %collective-permute-done.7.other = f32[32,2048]{1,0:T(8,128)S(1)} collective-permute-done((f32[32,2048]{1,0:T(8,128)S(1)}, f32[32,2048]{1,0:T(8,128)S(1)}, u32[]{:S(2)}, u32[]{:S(2)}) %collective-permute-start.7) | collective-permute-done | bytes 262176 | tf_op jit(solution)/shard_map/ppermute | solution.py:375
  93.3 0.7 finish.1
  94.0 0.1 reshape.50
  94.1 11.4 %all_to_all.16 = f32[8,4,2176]{2,1,0:T(4,128)S(1)} all-to-all(f32[8,4,2176]{2,1,0:T(4,128)S(1)} %reshape.50), channel_id=1, replica_groups=mesh['region'=32,'cols'=8] {'cols'}, dimensions={0} | all-to-all | bytes 557056 | tf_op jit(solution)/shard_map/all_to_all | solution.py:417
  105.5 0.1 broadcast_in_dim.31
  105.6 0.6 broadcast_in_dim.32
  106.2 11.9 %all-to-all-start.2 = ((f32[32,1,16]{2,1,0:T(1,128)}), f32[32,1,16]{2,1,0:T(1,128)S(1)}, u32[]{:S(2)}, u32[]{:S(2)}) async-start(f32[32,1,16]{2,1,0:T(1,128)} %broadcast_in_dim.32), calls=%async_computation.2 | async-start | bytes 32768 | tf_op jit(solution)/shard_map/all_to_all | solution.py:422
  118.2 8.4 %all-to-all-done.2 = f32[32,1,16]{2,1,0:T(1,128)S(1)} async-done(((f32[32,1,16]{2,1,0:T(1,128)}), f32[32,1,16]{2,1,0:T(1,128)S(1)}, u32[]{:S(2)}, u32[]{:S(2)}) %all-to-all-start.2) | async-done | bytes 2080 | tf_op jit(solution)/shard_map/all_to_all | solution.py:422
  126.6 0.1 reduce_sum.19
  126.7 0.1 reshape.51
  126.7 0.1 fusion.1
  126.8 0.2 fusion.4
  127.1 0.0 copy-done.6
  127.1 0.9 multiply_subtract_fusion
  (8 shorter events, 0.2 us)
Async XLA Ops:
  3.9 12.2 %all-to-all-start = ((f32[8,4,2176]{2,1,0:T(4,128)}), f32[8,4,2176]{2,1,0:T(4,128)S(1)}, u32[]{:S(2)}, u32[]{:S(2)}) async-start(f32[8,4,2176]{2,1,0:T(4,128)} %bitcast.5), calls=%async_computation | async-start | bytes 557056 | tf_op jit(solution)/shard_map/all_to_all | solution.py:391
  16.2 0.9 copy-start.2
  17.1 0.8 copy-start.3
  17.9 0.8 copy-start.4
  18.6 0.7 copy-start.5
  20.2 17.9 %collective-permute-start.2 = (f32[40,2176]{1,0:T(8,128)S(1)}, f32[40,2176]{1,0:T(8,128)S(1)}, u32[]{:S(2)}, u32[]{:S(2)}) collective-permute-start(f32[40,2176]{1,0:T(8,128)S(1)} %get-tuple-element.19.own.halo), channel_id=1, source_target_pairs={{2,0},{4,2},{6,4},{8,6},{10,8},{12,10},{14,12},{16,14},{18,16},{20... | collective-permute-start | bytes 1044488 | tf_op jit(solution)/shard_map/ppermute | solution.py:370
  23.9 25.9 %collective-permute-start.1 = (f32[40,2176]{1,0:T(8,128)S(1)}, f32[40,2176]{1,0:T(8,128)S(1)}, u32[]{:S(2)}, u32[]{:S(2)}) collective-permute-start(f32[40,2176]{1,0:T(8,128)S(1)} %get-tuple-element.19.own.halo), channel_id=1, source_target_pairs={{4,0},{6,2},{8,4},{10,6},{12,8},{14,10},{16,12},{18,14},{20,16},{2... | collective-permute-start | bytes 1044488 | tf_op jit(solution)/shard_map/ppermute | solution.py:370
  27.3 34.2 %collective-permute-start = (f32[40,2176]{1,0:T(8,128)S(1)}, f32[40,2176]{1,0:T(8,128)S(1)}, u32[]{:S(2)}, u32[]{:S(2)}) collective-permute-start(f32[40,2176]{1,0:T(8,128)S(1)} %get-tuple-element.19.own.halo), channel_id=1, source_target_pairs={{6,0},{8,2},{10,4},{12,6},{14,8},{16,10},{18,12},{20,14},{22,16},{... | collective-permute-start | bytes 1044488 | tf_op jit(solution)/shard_map/ppermute | solution.py:370
  35.4 2.0 %copy-start = (bf16[1024,2048]{1,0:T(8,128)(2,1)}, bf16[1024,2048]{1,0:T(8,128)(2,1)S(1)}, u32[]{:S(2)}) copy-start(bf16[1024,2048]{1,0:T(8,128)(2,1)S(1)} %get-tuple-element.34.low) | copy-start | bytes 12582916
  67.6 1.6 %collective-permute-start.3 = (f32[32,2048]{1,0:T(8,128)S(1)}, f32[32,2048]{1,0:T(8,128)S(1)}, u32[]{:S(2)}, u32[]{:S(2)}) collective-permute-start(f32[32,2048]{1,0:T(8,128)S(1)} %get-tuple-element.23.mine), channel_id=1, source_target_pairs={{0,1},{1,0},{2,3},{3,2},{4,5},{5,4},{6,7},{7,6},{8,9},{9,8},{10,11... | collective-permute-start | bytes 786440 | tf_op jit(solution)/shard_map/ppermute | solution.py:375
  69.3 11.9 %collective-permute-start.6 = (f32[32,2048]{1,0:T(8,128)S(1)}, f32[32,2048]{1,0:T(8,128)S(1)}, u32[]{:S(2)}, u32[]{:S(2)}) collective-permute-start(f32[32,2048]{1,0:T(8,128)S(1)} %get-tuple-element.26.vector), channel_id=1, source_target_pairs={{2,0},{4,2},{6,4},{8,6},{10,8},{12,10},{14,12},{16,14},{18,16},{20... | collective-permute-start | bytes 786440 | tf_op jit(solution)/shard_map/ppermute | solution.py:370
  72.5 14.9 %collective-permute-start.5 = (f32[32,2048]{1,0:T(8,128)S(1)}, f32[32,2048]{1,0:T(8,128)S(1)}, u32[]{:S(2)}, u32[]{:S(2)}) collective-permute-start(f32[32,2048]{1,0:T(8,128)S(1)} %get-tuple-element.26.vector), channel_id=1, source_target_pairs={{4,0},{6,2},{8,4},{10,6},{12,8},{14,10},{16,12},{18,14},{20,16},{2... | collective-permute-start | bytes 786440 | tf_op jit(solution)/shard_map/ppermute | solution.py:370
  75.4 15.0 %collective-permute-start.4 = (f32[32,2048]{1,0:T(8,128)S(1)}, f32[32,2048]{1,0:T(8,128)S(1)}, u32[]{:S(2)}, u32[]{:S(2)}) collective-permute-start(f32[32,2048]{1,0:T(8,128)S(1)} %get-tuple-element.26.vector), channel_id=1, source_target_pairs={{6,0},{8,2},{10,4},{12,6},{14,8},{16,10},{18,12},{20,14},{22,16},{... | collective-permute-start | bytes 786440 | tf_op jit(solution)/shard_map/ppermute | solution.py:370
  77.5 2.2 %copy-start.1 = (bf16[1024,2048]{1,0:T(8,128)(2,1)S(1)}, bf16[1024,2048]{1,0:T(8,128)(2,1)}, u32[]{:S(2)}) copy-start(bf16[1024,2048]{1,0:T(8,128)(2,1)} %copy-done) | copy-start | bytes 12582916
  90.4 36.7 %copy-start.6 = (f32[4,8192]{1,0:T(4,128)S(1)}, f32[4,8192]{1,0:T(4,128)}, u32[]{:S(2)}) copy-start(f32[4,8192]{1,0:T(4,128)} %param.7) | copy-start | bytes 393220
  91.7 1.6 %collective-permute-start.7 = (f32[32,2048]{1,0:T(8,128)S(1)}, f32[32,2048]{1,0:T(8,128)S(1)}, u32[]{:S(2)}, u32[]{:S(2)}) collective-permute-start(f32[32,2048]{1,0:T(8,128)S(1)} %apply3.1.mine), channel_id=1, source_target_pairs={{0,1},{1,0},{2,3},{3,2},{4,5},{5,4},{6,7},{7,6},{8,9},{9,8},{10,11... | collective-permute-start | bytes 786440 | tf_op jit(solution)/shard_map/ppermute | solution.py:375
  106.2 20.4 %all-to-all-start.2 = ((f32[32,1,16]{2,1,0:T(1,128)}), f32[32,1,16]{2,1,0:T(1,128)S(1)}, u32[]{:S(2)}, u32[]{:S(2)}) async-start(f32[32,1,16]{2,1,0:T(1,128)} %broadcast_in_dim.32), calls=%async_computation.2 | async-start | bytes 32768 | tf_op jit(solution)/shard_map/all_to_all | solution.py:422

commit v2 on v1

v2 whole, which is shorter than its diff:
```python
import functools

import jax
import jax.numpy as jnp
from jax import lax
from jax.experimental import pallas as pl
from jax.experimental.pallas import tpu as pltpu
from jax.sharding import PartitionSpec as P

BLOCK = 256
KMAX = 23
SUPPORT = 1000.0 / 6371.0

STRETCH = 4.0**0.2
TOP = 5.0 / STRETCH**4
GAMMA = 2.0 * STRETCH**2 / SUPPORT**2
FAR = 2.0**100

ROWS = 32
CHIP = 8 * BLOCK
HALF = 4 * BLOCK
WIDE = CHIP + 128
AXES = ("region", "cols")

bf16 = jnp.bfloat16
f32 = jnp.float32


def dot(a, b):
    return jnp.dot(a, b, preferred_element_type=f32)


def two_parts(x):
    high = x.astype(bf16)
    return high, (x - high.astype(f32)).astype(bf16)


def three_parts(x):
    first = x.astype(bf16).astype(f32)
    rest = x - first
    second = rest.astype(bf16).astype(f32)
    return first, second, (rest - second).astype(bf16).astype(f32)


def vmem(count):
    return [pl.BlockSpec(memory_space=pltpu.VMEM)] * count


def smem(count):
    return [pl.BlockSpec(memory_space=pltpu.SMEM)] * count


def hbm(count):
    return [pl.BlockSpec(memory_space=pltpu.HBM)] * count


def in_hbm(array):
    return pltpu.with_memory_space_constraint(array, pltpu.HBM)


def params(mebibytes):
    return pltpu.CompilerParams(vmem_limit_bytes=mebibytes * 1024 * 1024)


def chip_at(place, row_at):
    turned = row_at ^ (2 * place[3])
    return turned ^ (turned >> 1)


def split_kernel(
    place, count, pairs, innovations, own, ahead1, ahead2, ahead3, held, sems
):
    copies = [pltpu.make_async_copy(pairs, held, sems.at[4])]
    outs = (own, ahead1, ahead2, ahead3)
    for step, out in enumerate(outs):
        at = chip_at(place, (place[2] + step) & 3) * CHIP
        source = innovations.at[:, pl.ds(pl.multiple_of(at, CHIP), CHIP)]
        copies.append(
            pltpu.make_async_copy(source, out.at[:, pl.ds(0, CHIP)], sems.at[step])
        )
    for copy in copies:
        copy.start()
    copies[0].wait()
    left, right = held[0:1, :], held[1:2, :]
    slot = lax.broadcasted_iota(jnp.int32, left.shape, 1)
    live = jnp.where(slot < count[0], left * 24 + (right - left), -1).astype(f32)
    for copy in copies[1:]:
        copy.wait()
    for out in outs:
        out[:, CHIP:] = jnp.full((4, 128), -1.0, f32)
        out[0:1, CHIP : CHIP + live.shape[1]] = live


def split(place, count, pairs, innovations):
    part = jax.ShapeDtypeStruct((4, WIDE), f32)
    return pl.pallas_call(
        split_kernel,
        out_shape=(part, part, part, part),
        in_specs=smem(2) + hbm(2),
        out_specs=vmem(4),
        scratch_shapes=[
            pltpu.VMEM(pairs.shape, jnp.int32),
            pltpu.SemaphoreType.DMA((5,)),
        ],
        compiler_params=params(4),
        name="split",
    )(place, count, in_hbm(pairs), in_hbm(innovations))


def assemble_kernel(place, own, behind1, behind2, behind3, out):
    for y in range(4):
        step = (place[2] - y) & 3
        value = jnp.where(step == 0, own[...], behind1[...])
        value = jnp.where(step == 2, behind2[...], value)
        value = jnp.where(step == 3, behind3[...], value)
        out[4 * y : 4 * y + 4, :] = value


def assemble(place, own, behind1, behind2, behind3):
    return pl.pallas_call(
        assemble_kernel,
        out_shape=jax.ShapeDtypeStruct((16, WIDE), f32),
        in_specs=smem(1) + vmem(4),
        out_specs=vmem(1)[0],
        compiler_params=params(4),
        name="assemble",
    )(place, own, behind1, behind2, behind3)


def pair_flags(row_at, core, mine, other):
    sub = lax.broadcasted_iota(jnp.int32, (8, 128), 0)
    col = lax.broadcasted_iota(jnp.int32, (8, 128), 1)
    far = col < 24
    near = col - lax.div(col, 8) * 8
    ahead = 8 * (lax.div(col, 8) + 1)
    offset = jnp.where(far, ahead + sub - near, jnp.abs(near - sub))
    left_up = jnp.where(far, near, jnp.minimum(near, sub))
    left_down = jnp.where(far, 7 - sub, 7 - jnp.maximum(near, sub))
    left = jnp.where(core == 0, left_up, left_down)
    valid = (offset >= 0) & (offset <= KMAX) & (col < 32)
    target = jnp.where(valid, (row_at * 8 + left) * 24 + offset, -7).astype(f32)
    hit = jnp.zeros((8, 128), f32)
    for source in (mine, other):
        known = source[0:1, CHIP:]
        for y in (1, 2, 3):
            known = jnp.where(row_at == y, source[4 * y : 4 * y + 1, CHIP:], known)
        for i in range(96):
            code = jnp.broadcast_to(known[0:1, i : i + 1], (8, 128))
            hit = jnp.where(code == target, 1.0, hit)
    return jnp.where(hit > 0.5, 0.0, FAR)


def points_kernel(
    place,
    counts,
    all_coords,
    all_std,
    all_variance,
    base,
    aux,
    first,
    right,
    coords,
    std,
    variance,
    sems,
):
    row_at, core = place[0], place[1]
    chip = pl.ds(pl.multiple_of(row_at * CHIP, CHIP), CHIP)
    copies = [
        pltpu.make_async_copy(source.at[:, chip], to, sems.at[i])
        for i, (source, to) in enumerate(
            ((all_coords, coords), (all_std, std), (all_variance, variance))
        )
    ]
    for copy in copies:
        copy.start()
    base[...] = jnp.zeros((8, CHIP), f32)
    for copy in copies:
        copy.wait()
    lane = lax.broadcasted_iota(jnp.int32, (1, BLOCK), 1)
    for j in range(8):
        source = j + core * (7 - 2 * j)
        here = slice(j * BLOCK, (j + 1) * BLOCK)
        region = pl.ds(pl.multiple_of(source * BLOCK, BLOCK), BLOCK)
        live = (lane < counts[row_at * 8 + source]).astype(f32)
        base[0:3, here] = coords[:, region]
        aux[0:1, here] = std[0:1, region] * live
        aux[1:2, here] = variance[0:1, region]
    sub = lax.broadcasted_iota(jnp.int32, (8, CHIP), 0)
    points = base[...]
    side = jnp.where(sub < 3, points * (-GAMMA), jnp.where(sub == 3, GAMMA, 0.0))
    a1, a2, a3 = three_parts(side)
    first[...] = a1
    right[0:16, :] = jnp.concatenate([a2, a2], 0).astype(bf16)
    right[16:32, :] = jnp.concatenate([a1, a3], 0).astype(bf16)


def points(place, counts, coords, std, variance):
    return pl.pallas_call(
        points_kernel,
        out_shape=(
            jax.ShapeDtypeStruct((8, CHIP), f32),
            jax.ShapeDtypeStruct((8, CHIP), f32),
            jax.ShapeDtypeStruct((8, CHIP), f32),
            jax.ShapeDtypeStruct((32, CHIP), bf16),
        ),
        in_specs=smem(2) + hbm(3),
        out_specs=vmem(4),
        scratch_shapes=[
            pltpu.VMEM((3, CHIP), f32),
            pltpu.VMEM((1, CHIP), f32),
            pltpu.VMEM((1, CHIP), f32),
            pltpu.SemaphoreType.DMA((3,)),
        ],
        compiler_params=params(4),
        name="points",
    )(place, counts, in_hbm(coords), in_hbm(std), in_hbm(variance))


def vectors_kernel(place, mine, other, base, aux, halo, vector, flags):
    core = place[1]
    pairs = pair_flags(place[0], core, mine, other)
    flags[...] = pairs
    halo[32:40, 0:CHIP] = base[...]
    halo[32:40, CHIP:] = pairs
    halo[0:32, CHIP:] = jnp.zeros((32, 128), f32)
    for j in range(8):
        here = slice(j * BLOCK, (j + 1) * BLOCK)
        source = (j + core * (7 - 2 * j)) * BLOCK
        local = pl.ds(pl.multiple_of(source, BLOCK), BLOCK)
        spread = aux[0:1, here]
        got, had = other[:, local], mine[:, local]
        for y in range(4):
            rows = slice(4 * y, 4 * y + 4)
            up = jnp.concatenate([had[rows], got[rows]], 0)
            down = jnp.concatenate([got[rows], had[rows]], 0)
            value = jnp.where(core == 0, up, down)
            vector[8 * y : 8 * y + 8, here] = value
            halo[8 * y : 8 * y + 8, here] = value * spread


def vectors(place, mine, other, base, aux):
    return pl.pallas_call(
        vectors_kernel,
        out_shape=(
            jax.ShapeDtypeStruct((40, WIDE), f32),
            jax.ShapeDtypeStruct((ROWS, CHIP), f32),
            jax.ShapeDtypeStruct((8, 128), f32),
        ),
        in_specs=smem(1) + vmem(4),
        out_specs=vmem(3),
        compiler_params=params(4),
        name="vectors",
    )(place, mine, other, base, aux)


def distance(left, right):
    return jnp.maximum(dot(left, right), 1e-30)


def covariance(x):
    z = jnp.maximum(STRETCH - x * lax.rsqrt(x), 0.0)
    z2 = z * z
    return z2 * z2 * (TOP - z)


def sides(count, offset, place, own, halo, first, mask, left, top):
    column = 24 if offset == 0 else 8 * (offset - 1)
    flags = jnp.where(place[1] == 0, own[...], halo[32:40, CHIP:])
    for a in range(8):
        mask[:, a * BLOCK : (a + 1) * BLOCK] = jnp.broadcast_to(
            flags[:, column + a : column + a + 1], (8, BLOCK)
        )
    width = count * BLOCK
    sub = lax.broadcasted_iota(jnp.int32, (8, width), 0)
    points = halo[32:40, 0:width]
    b1, b2, b3 = three_parts(
        jnp.where(sub < 3, points, jnp.where(sub < 5, 1.0, 0.0))
    )
    left[0:width, :] = jnp.concatenate([b1, b2, b1, b2, b3, b1], 0).T.astype(bf16)
    sub = lax.broadcasted_iota(jnp.int32, (8, CHIP), 0)
    a1 = first[...]
    for b in range(count):
        row = jnp.broadcast_to(mask[b : b + 1, :], (8, CHIP))
        top[16 * b : 16 * b + 16, :] = jnp.concatenate(
            [jnp.where(sub == 4, row, a1), a1], 0
        ).astype(bf16)


def side_scratch(count):
    return [
        pltpu.VMEM((8, CHIP), f32),
        pltpu.VMEM((count * BLOCK, 48), bf16),
        pltpu.VMEM((count * 16, CHIP), bf16),
        pltpu.VMEM((2, BLOCK, BLOCK), f32),
    ]


def make_tiles(jobs, left, top, right, high, low, held, total=None):
    def start(n):
        block, here, _, _, _ = jobs[n]
        rows = pl.ds(pl.multiple_of(block * BLOCK, BLOCK), BLOCK)
        upper = pl.ds(pl.multiple_of(block * 16, 16), 16)
        side = jnp.concatenate([top[upper, here], right[:, here]], 0)
        held[n % 2] = distance(left[rows, :], side)

    start(0)
    for n, (_, here, rows, columns, parts) in enumerate(jobs):
        if n + 1 < len(jobs):
            start(n + 1)
        value = covariance(held[n % 2])
        th = value.astype(bf16)
        high[rows, columns] = th
        tl = (value - th.astype(f32)).astype(bf16)
        low[rows, columns] = tl
        if total is not None:
            pair = dot(jnp.concatenate(parts, 0), th)
            total[:, here] += (pair[0:ROWS] + pair[ROWS:]) + dot(parts[0], tl)


def tiles0_kernel(place, own, halo, first, right, high, low, mask, left, top, held):
    sides(4, 0, place, own, halo, first, mask, left, top)
    jobs = []
    for b in range(4):
        for a in range(8):
            here = slice(a * BLOCK, (a + 1) * BLOCK)
            jobs.append((b, here, slice(b * BLOCK, (b + 1) * BLOCK), here, None))
    make_tiles(jobs, left, top, right, high, low, held)


def tiles0(place, own, halo, first, right):
    kept = pltpu.VMEM((HALF, CHIP), bf16)
    return pl.pallas_call(
        tiles0_kernel,
        out_shape=(kept, kept),
        in_specs=smem(1) + vmem(4),
        out_specs=vmem(2),
        scratch_shapes=side_scratch(4),
        compiler_params=params(5),
        name="tiles0",
    )(place, own, halo, first, right)


def tiles_kernel(
    offset,
    place,
    own,
    halo,
    first,
    right,
    before,
    high,
    low,
    total,
    mask,
    left,
    top,
    held,
):
    sides(8, offset, place, own, halo, first, mask, left, top)
    total[...] = before[...]

    def four_blocks(i, carry):
        jobs = []
        for n in range(4):
            b = 4 * i + n
            rows = pl.ds(pl.multiple_of(b * BLOCK, BLOCK), BLOCK)
            parts = two_parts(halo[0:ROWS, rows])
            for a in range(8):
                here = slice(a * BLOCK, (a + 1) * BLOCK)
                jobs.append((b, here, rows, here, parts))
        make_tiles(jobs, left, top, right, high, low, held, total)
        return carry

    lax.fori_loop(0, 2, four_blocks, 0)


def tiles(offset, place, own, halo, first, right, before):
    kept = pltpu.VMEM((CHIP, CHIP), bf16)
    return pl.pallas_call(
        functools.partial(tiles_kernel, offset),
        out_shape=(kept, kept, jax.ShapeDtypeStruct((ROWS, CHIP), f32)),
        in_specs=smem(1) + vmem(5),
        out_specs=vmem(3),
        scratch_shapes=side_scratch(8),
        compiler_params=params(6),
        name=f"tiles{offset}",
    )(place, own, halo, first, right, before)


def edge_kernel(
    place, own, halo, first, right, before, high, low, total, mask, left, top, held
):
    sides(7, 3, place, own, halo, first, mask, left, top)
    total[...] = before[...]
    jobs = []
    for j in range(7):
        rows = slice(j * BLOCK, (j + 1) * BLOCK)
        parts = two_parts(halo[0:ROWS, rows])
        for a in range(j + 1, 8):
            here = slice(a * BLOCK, (a + 1) * BLOCK)
            at = (a * (a - 1) // 2 + j) * BLOCK
            jobs.append((j, here, slice(at, at + BLOCK), slice(0, BLOCK), parts))
    make_tiles(jobs, left, top, right, high, low, held, total)


def edge_tiles(place, own, halo, first, right, before):
    kept = pltpu.VMEM((28 * BLOCK, BLOCK), bf16)
    return pl.pallas_call(
        edge_kernel,
        out_shape=(kept, kept, jax.ShapeDtypeStruct((ROWS, CHIP), f32)),
        in_specs=smem(1) + vmem(5),
        out_specs=vmem(3),
        scratch_shapes=side_scratch(7),
        compiler_params=params(6),
        name="tiles3",
    )(place, own, halo, first, right, before)


def apply_kernel(depth, vector, high, low, before, total):
    uh, ul = two_parts(vector[0:32, 0:depth])
    both = jnp.concatenate([uh, ul], 0)
    for n in range(0, CHIP, 512):
        here = slice(n, n + 512)
        pair = dot(both, high[:, here])
        extra = dot(uh, low[:, here])
        total[:, here] = before[:, here] + ((pair[0:32] + pair[32:64]) + extra)


def apply(vector, high, low, before):
    depth = high.shape[0]
    return pl.pallas_call(
        functools.partial(apply_kernel, depth),
        out_shape=jax.ShapeDtypeStruct((ROWS, CHIP), f32),
        in_specs=vmem(4),
        out_specs=vmem(1)[0],
        compiler_params=params(8),
        name="apply",
    )(vector, high, low, before)


def edge_apply_kernel(vector, high, low, before, total):
    uh, ul = two_parts(vector[0:32, 0 : 7 * BLOCK])
    both = jnp.concatenate([uh, ul], 0)
    total[:, 0:BLOCK] = before[:, 0:BLOCK]
    for a in range(1, 8):
        rows = slice(a * (a - 1) // 2 * BLOCK, a * (a + 1) // 2 * BLOCK)
        here = slice(a * BLOCK, (a + 1) * BLOCK)
        pair = dot(both[:, 0 : a * BLOCK], high[rows, :])
        extra = dot(uh[:, 0 : a * BLOCK], low[rows, :])
        total[:, here] = before[:, here] + ((pair[0:32] + pair[32:64]) + extra)


def edge_apply(vector, high, low, before):
    return pl.pallas_call(
        edge_apply_kernel,
        out_shape=jax.ShapeDtypeStruct((ROWS, CHIP), f32),
        in_specs=vmem(4),
        out_specs=vmem(1)[0],
        compiler_params=params(8),
        name="apply3",
    )(vector, high, low, before)


def combine_kernel(mine, other, aux, vector, image, scaled):
    for j in range(8):
        here = slice(j * BLOCK, (j + 1) * BLOCK)
        there = slice((7 - j) * BLOCK, (8 - j) * BLOCK)
        spread = aux[0:1, here]
        value = (mine[:, here] + other[:, there]) * spread
        value = value + aux[1:2, here] * vector[:, here]
        image[:, here] = value
        scaled[:, here] = value * spread


def combine(mine, other, aux, vector):
    shape = jax.ShapeDtypeStruct((ROWS, CHIP), f32)
    return pl.pallas_call(
        combine_kernel,
        out_shape=(shape, shape),
        in_specs=vmem(4),
        out_specs=vmem(2),
        compiler_params=params(8),
        name="combine",
    )(mine, other, aux, vector)


def finish_kernel(
    place, mine, other, aux, vector, image, own, ahead1, ahead2, ahead3, last, packed
):
    row_at, core = place[2], place[1]
    sums = [jnp.zeros((ROWS, 1), f32) for _ in range(4)]
    for j in range(8):
        here = slice(j * BLOCK, (j + 1) * BLOCK)
        there = slice((7 - j) * BLOCK, (8 - j) * BLOCK)
        start, first = vector[:, here], image[:, here]
        value = (mine[:, here] + other[:, there]) * aux[0:1, here]
        value = value + aux[1:2, here] * first
        last[:, here] = value
        terms = (start * start, start * first, first * first, first * value)
        sums = [s + jnp.sum(t, axis=1, keepdims=True) for s, t in zip(sums, terms)]
    lane = lax.broadcasted_iota(jnp.int32, (ROWS, 128), 1)
    row = jnp.zeros((ROWS, 128), f32)
    for i in range(4):
        row = jnp.where(lane == i, sums[i], row)
    packed[...] = row
    for step, out in enumerate((own, ahead1, ahead2, ahead3)):
        rows = pl.ds(pl.multiple_of(lax.rem(row_at + step, 4) * 8, 8), 8)

        def chosen(value):
            return jnp.where(core == 0, value[0:4], value[4:8])

        for j in range(8):
            here = slice(j * BLOCK, (j + 1) * BLOCK)
            to = (j + core * (7 - 2 * j)) * BLOCK
            out[:, pl.ds(pl.multiple_of(to, BLOCK), BLOCK)] = chosen(image[rows, here])
            out[:, pl.ds(pl.multiple_of(CHIP + to, BLOCK), BLOCK)] = chosen(
                last[rows, here]
            )
        out[:, 2 * CHIP :] = chosen(packed[rows, :])


def finish(place, mine, other, aux, vector, image):
    part = jax.ShapeDtypeStruct((4, 2 * CHIP + 128), f32)
    return pl.pallas_call(
        finish_kernel,
        out_shape=(part, part, part, part),
        in_specs=smem(1) + vmem(5),
        out_specs=vmem(4),
        scratch_shapes=[pltpu.VMEM((ROWS, CHIP), f32), pltpu.VMEM((ROWS, 128), f32)],
        compiler_params=params(6),
        name="finish",
    )(place, mine, other, aux, vector, image)


def region_sums_kernel(own, behind1, behind2, behind3, out):
    total = own[:, 2 * CHIP :] + behind1[:, 2 * CHIP :]
    total = total + (behind2[:, 2 * CHIP :] + behind3[:, 2 * CHIP :])
    out[...] = jnp.broadcast_to(total[None], out.shape)


def region_sums(regions, parts):
    return pl.pallas_call(
        region_sums_kernel,
        out_shape=jax.ShapeDtypeStruct((regions, 4, 128), f32),
        in_specs=vmem(4),
        out_specs=vmem(1)[0],
        compiler_params=params(6),
        name="region_sums",
    )(*parts)


def result_kernel(
    place, sums, innovations, own, behind1, behind2, behind3, field, residual
):
    totals = jnp.sum(sums[...], axis=0)
    bb, bk, kk, kl = (totals[:, i : i + 1] for i in range(4))
    alpha = bb / bk
    norm = alpha * alpha * kk - 2.0 * alpha * bk + bb
    grown = 1.0 + norm / bb
    energy = grown * grown * bk - 2.0 * alpha * grown * kk + alpha * alpha * kl
    step = norm / energy
    for back, part in enumerate((own, behind1, behind2, behind3)):
        at = chip_at(place, (place[2] - back) & 3) * CHIP
        here = pl.ds(pl.multiple_of(at, CHIP), CHIP)
        start = innovations[:, here]
        first, last = part[:, 0:CHIP], part[:, CHIP : 2 * CHIP]
        field[:, here] = alpha * start + step * (grown * start - alpha * first)
        residual[:, here] = (
            start - alpha * first - step * (grown * first - alpha * last)
        )


def result(place, sums, innovations, parts):
    shape = jax.ShapeDtypeStruct(innovations.shape, f32)
    return pl.pallas_call(
        result_kernel,
        out_shape=(shape, shape),
        in_specs=smem(1) + vmem(6),
        out_specs=vmem(2),
        compiler_params=params(6),
        name="result",
    )(place, sums, innovations, *parts)


def device(chip, core):
    region, place = divmod(chip, 4)
    return 8 * region + 2 * (place ^ (place >> 1) ^ (2 * (region % 2))) + core


def neighbours(block, step, chips):
    route = []
    for m in range(chips - step):
        route.append((device(m + step, 0), device(m, 0)))
        route.append((device(m, 1), device(m + step, 1)))
    return lax.ppermute(block, AXES, route)


def sibling(block, chips):
    route = [(i, i ^ 1) for i in range(2 * chips)]
    return lax.ppermute(block, AXES, route)


after = lax.optimization_barrier


def along_y(parts):
    columns = lax.axis_size("cols")
    return [
        lax.ppermute(
            part, "cols", [(i, (i + 2 * step) % columns) for i in range(columns)]
        )
        for step, part in enumerate(parts, 1)
    ]


def per_device(
    innovations, coords, background_std, obs_variance, block_count, pair_list, pair_count
):
    regions = lax.axis_size("region")
    chips = regions * lax.axis_size("cols") // 2
    column = lax.axis_index("cols")
    row_at = column // 2
    odd = lax.axis_index("region") % 2
    turned = row_at ^ (2 * odd)
    place = jnp.stack([turned ^ (turned >> 1), column % 2, row_at, odd])

    own, *ahead = split(place, pair_count, pair_list, innovations)
    behind = along_y(ahead)
    base, aux, first, right = points(
        place,
        block_count,
        coords,
        background_std.reshape(1, -1),
        obs_variance.reshape(1, -1),
    )
    half = assemble(place, own, *behind)
    halo, vector, flags = vectors(place, half, sibling(half, chips), base, aux)

    halos = [neighbours(halo, step, chips) for step in (1, 2, 3)]
    kept = [tiles0(place, flags, halo, first, right)]
    total = apply(halo, *kept[0], jnp.zeros((ROWS, CHIP), f32))
    for k in (1, 2):
        *made, total = tiles(k, place, flags, halos[k - 1], first, right, total)
        kept.append(made)
    *made, part = edge_tiles(place, flags, halos[2], first, right, total)
    kept.append(made)
    image, scaled = combine(part, sibling(part, chips), aux, vector)

    halos = [scaled] + [neighbours(scaled, step, chips) for step in (1, 2, 3)]
    total = jnp.zeros((ROWS, CHIP), f32)
    for k in range(3):
        total = apply(halos[k], *kept[k], total)
    part = edge_apply(halos[3], *kept[3], total)
    own, *ahead = finish(place, part, sibling(part, chips), aux, vector, image)

    parts = [own] + along_y(ahead)
    sums = lax.all_to_all(region_sums(regions, parts), "region", 0, 0, tiled=True)
    return result(place, sums, innovations, parts)


def solution(mesh):
    placed = (
        P("cols", "region"),
        P(None, "region"),
        P("region"),
        P("region"),
        P("region"),
        P(None, ("region", "cols")),
        P(("region", "cols")),
    )
    return jax.shard_map(
        per_device,
        mesh=mesh,
        in_specs=placed,
        out_specs=(P("cols", "region"), P("cols", "region")),
        check_vma=False,
    )
```

time: 129 us -> 112 us (0.87)
  waiting for transfers between devices: 23.1 us -> 8.11 us
  local copies, waits for them, and re-layouts: 10.1 us -> 0.67 us
  blocking collectives: 11.4 us -> 19.7 us
  other arithmetic: 2.14 us -> 0.08 us
  starting transfers between devices: 33.6 us -> 35.3 us
    all_to_all x2 -> x0, starting transfers between devices: 16.4 us -> none  [the longest x1 11.9 us: per_device(): lax.all_to_all(jnp.broadcast_to(sums.reshape(1, 16), (regions, 16)), 'reg...]
    all_to_all x2 -> x0, waiting for transfers between devices: 16.1 us -> none  [the longest x1 8.42 us: per_device(): lax.all_to_all(jnp.broadcast_to(sums.reshape(1, 16), (regions, 16)), 'reg...]
    ppermute x0 -> x6, starting transfers between devices: none -> 11.8 us  [along_y(): lax.ppermute(part, 'cols', [(i, (i + 2 * step) % columns) for i in range(...]
    all_to_all x1, blocking collectives: 11.4 us -> 19.7 us  [per_device(): lax.all_to_all(region_sums(regions, parts), 'region', 0, 0, tiled=True)]
    unnamed x14 -> x4, local copies, waits for them, and re-layouts: 7.21 us -> 0.65 us
    ppermute x6, starting transfers between devices: 17.1 us -> 23 us  [neighbours(): return lax.ppermute(block, AXES, route)]
    ppermute x0 -> x6, waiting for transfers between devices: none -> 5.12 us  [along_y(): lax.ppermute(part, 'cols', [(i, (i + 2 * step) % columns) for i in range(...]
    ppermute x6, waiting for transfers between devices: 3.98 us -> 0.27 us  [neighbours(): return lax.ppermute(block, AXES, route)]
  transfers between devices with their start and end apart: 10 -> 15, of which waited for: 6 -> 7; matrix products, arithmetic and copies ran while one was open for 0% -> 0% of each run, Pallas kernels for 29% -> 31%
where the time goes in v2:
time: 112 us
  Pallas kernels  46.4 us (41%)
  starting transfers between devices  35.3 us (32%)
  blocking collectives  19.7 us (18%)
  waiting for transfers between devices  8.11 us (7%)
  between operations  1.51 us (1%)
    ppermute x6, starting transfers between devices, neighbours(): return lax.ppermute(block, AXES, route)  23 us
    all_to_all x1, blocking collectives, per_device(): lax.all_to_all(region_sums(regions, parts), 'region', 0, 0, tiled=True)  19.7 us
    pallas_call x2, Pallas kernels, tiles(): pl.pallas_call(functools.partial(tiles_kernel, offset), out_shape=(kept,...  19.6 us
    ppermute x6, starting transfers between devices, along_y(): lax.ppermute(part, 'cols', [(i, (i + 2 * step) % columns) for i in range(...  11.8 us
    pallas_call x4, Pallas kernels, apply(): pl.pallas_call(functools.partial(apply_kernel, depth), out_shape=jax.Shap...  9.1 us
    ppermute x6, waiting for transfers between devices, along_y(): lax.ppermute(part, 'cols', [(i, (i + 2 * step) % columns) for i in range(...  5.12 us
    pallas_call x1, Pallas kernels, tiles0(): pl.pallas_call(tiles0_kernel, out_shape=(kept, kept), in_specs=smem(1) +...  4.96 us
    pallas_call x1, Pallas kernels, edge_tiles(): pl.pallas_call(edge_kernel, out_shape=(kept, kept, jax.ShapeDtypeStruct((...  4.71 us
  transfers between devices with their start and end apart: 15, of which 7 were waited for; matrix products, arithmetic and copies ran while one was open for 0% of the time, Pallas kernels for 31%

profile of v2, /device:TPU:2, one launch (start us, length us, event | category | flops | bytes accessed | tf_op | source)
XLA Modules:
  0.0 111.8 jit_solution(932900511438775808)
XLA Ops:
  1.3 0.1 pad_add_fusion.place
  1.4 1.4 %split.1 = (f32[4,2176]{1,0:T(4,128)S(1)}, f32[4,2176]{1,0:T(4,128)S(1)}, f32[4,2176]{1,0:T(4,128)S(1)}, f32[4,2176]{1,0:T(4,128)S(1)}) custom-call(s32[4]{0:T(128)S(1)} %pad_add_fusion.place, s32[1]{0:T(128)S(6)} %copy.9.count, s32[2,96]{1,0:T(2,128)} %pairs.1, f32[4,8192]{1,0:T(4,128)} %innovations.3), custom_call_target="tpu_custom_call" | custom-call | tf_op jit(solution)/shard_map/split/pallas_call | solution.py:96
  2.8 1.7 %collective-permute-start = (f32[4,2176]{1,0:T(4,128)S(1)}, f32[4,2176]{1,0:T(4,128)S(1)}, u32[]{:S(2)}, u32[]{:S(2)}) collective-permute-start(f32[4,2176]{1,0:T(4,128)S(1)} %get-tuple-element.31), channel_id=1, source_target_pairs={{0,2},{1,3},{2,4},{3,5},{4,6},{5,7},{6,0},{7,1},{8,10},{9,11},{10,... | collective-permute-start | bytes 104456 | tf_op jit(solution)/shard_map/ppermute | solution.py:611
  4.5 2.9 %collective-permute-start.1 = (f32[4,2176]{1,0:T(4,128)S(1)}, f32[4,2176]{1,0:T(4,128)S(1)}, u32[]{:S(2)}, u32[]{:S(2)}) collective-permute-start(f32[4,2176]{1,0:T(4,128)S(1)} %get-tuple-element.32), channel_id=1, source_target_pairs={{0,4},{1,5},{2,6},{3,7},{4,0},{5,1},{6,2},{7,3},{8,12},{9,13},{10,... | collective-permute-start | bytes 104456 | tf_op jit(solution)/shard_map/ppermute | solution.py:611
  7.4 1.3 %collective-permute-start.2 = (f32[4,2176]{1,0:T(4,128)S(1)}, f32[4,2176]{1,0:T(4,128)S(1)}, u32[]{:S(2)}, u32[]{:S(2)}) collective-permute-start(f32[4,2176]{1,0:T(4,128)S(1)} %get-tuple-element.33), channel_id=1, source_target_pairs={{0,6},{1,7},{2,0},{3,1},{4,2},{5,3},{6,4},{7,5},{8,14},{9,15},{10,... | collective-permute-start | bytes 104456 | tf_op jit(solution)/shard_map/ppermute | solution.py:611
  8.7 0.0 collective-permute-done.behind1
  8.7 1.2 %collective-permute-done.1.behind2 = f32[4,2176]{1,0:T(4,128)S(1)} collective-permute-done((f32[4,2176]{1,0:T(4,128)S(1)}, f32[4,2176]{1,0:T(4,128)S(1)}, u32[]{:S(2)}, u32[]{:S(2)}) %collective-permute-start.1) | collective-permute-done | bytes 34848 | tf_op jit(solution)/shard_map/ppermute | solution.py:611
  9.9 1.4 %collective-permute-done.2.behind3 = f32[4,2176]{1,0:T(4,128)S(1)} collective-permute-done((f32[4,2176]{1,0:T(4,128)S(1)}, f32[4,2176]{1,0:T(4,128)S(1)}, u32[]{:S(2)}, u32[]{:S(2)}) %collective-permute-start.2) | collective-permute-done | bytes 34848 | tf_op jit(solution)/shard_map/ppermute | solution.py:611
  11.3 0.6 assemble.1.mine
  11.9 0.1 collective-permute-start.3
  12.0 0.0 copy-start.1
  12.0 0.6 copy-done.1
  12.6 1.4 %points.1 = (f32[8,2048]{1,0:T(8,128)S(1)}, f32[8,2048]{1,0:T(8,128)S(1)}, f32[8,2048]{1,0:T(8,128)S(1)}, bf16[32,2048]{1,0:T(8,128)(2,1)S(1)}) custom-call(s32[4]{0:T(128)S(1)} %pad_add_fusion.place, s32[32]{0:T(128)S(1)} %copy-done.1, f32[3,8192]{1,0:T(4,128)} %all_coords.1, f32[1,8192]{1,0:T(1,128)} %bitcast.6, f32[1,8192]{1,0:T(1,128)} %bitcast.7), custom_call_target="tpu_custom_call" | custom-call | tf_op jit(solution)/shard_map/points/pallas_call | solution.py:200
  14.0 0.0 collective-permute-done.3.other
  14.0 0.9 vectors.1
  15.0 2.1 %collective-permute-start.6 = (f32[40,2176]{1,0:T(8,128)S(1)}, f32[40,2176]{1,0:T(8,128)S(1)}, u32[]{:S(2)}, u32[]{:S(2)}) collective-permute-start(f32[40,2176]{1,0:T(8,128)S(1)} %get-tuple-element.37.halo.vector), channel_id=1, source_target_pairs={{2,0},{1,3},{6,2},{3,7},{4,6},{7,5},{12,4},{5,13},{14,12},{13,15},... | collective-permute-start | bytes 1044488 | tf_op jit(solution)/shard_map/ppermute | solution.py:597
  17.1 4.3 %collective-permute-start.5 = (f32[40,2176]{1,0:T(8,128)S(1)}, f32[40,2176]{1,0:T(8,128)S(1)}, u32[]{:S(2)}, u32[]{:S(2)}) collective-permute-start(f32[40,2176]{1,0:T(8,128)S(1)} %get-tuple-element.37.halo.vector), channel_id=1, source_target_pairs={{6,0},{1,7},{4,2},{3,5},{12,6},{7,13},{14,4},{5,15},{10,12},{13,11... | collective-permute-start | bytes 1044488 | tf_op jit(solution)/shard_map/ppermute | solution.py:597
  21.4 4.8 %collective-permute-start.4 = (f32[40,2176]{1,0:T(8,128)S(1)}, f32[40,2176]{1,0:T(8,128)S(1)}, u32[]{:S(2)}, u32[]{:S(2)}) collective-permute-start(f32[40,2176]{1,0:T(8,128)S(1)} %get-tuple-element.37.halo.vector), channel_id=1, source_target_pairs={{4,0},{1,5},{12,2},{3,13},{14,6},{7,15},{10,4},{5,11},{8,12},{13,9... | collective-permute-start | bytes 1044488 | tf_op jit(solution)/shard_map/ppermute | solution.py:597
  26.2 5.0 %tiles0.1 = (bf16[1024,2048]{1,0:T(8,128)(2,1)S(1)}, bf16[1024,2048]{1,0:T(8,128)(2,1)S(1)}) custom-call(s32[4]{0:T(128)S(1)} %pad_add_fusion.place, f32[8,128]{1,0:T(8,128)S(1)} %get-tuple-element.36.own, f32[40,2176]{1,0:T(8,128)S(1)} %get-tuple-element.37.halo.vector, f32[8,2048]{1,0:T(8,128)S(1)} %get-tuple-element.38.first, ...), custom_call_target="tpu_custom_call" | custom-call | tf_op jit(solution)/shard_map/tiles0/pallas_call | solution.py:334
  31.2 1.5 %apply.4.before = f32[32,2048]{1,0:T(8,128)S(1)} custom-call(f32[40,2176]{1,0:T(8,128)S(1)} %get-tuple-element.37.halo.vector, bf16[1024,2048]{1,0:T(8,128)(2,1)S(1)} %get-tuple-element.40.high, bf16[1024,2048]{1,0:T(8,128)(2,1)S(1)} %get-tuple-element.41.low, f32[32,2048]{1,0:T(8,128)S(1)} %broadcast_1_before.2.before), custom_call_target="tpu_custom_call" | custom-call | tf_op jit(solution)/shard_map/apply/pallas_call | solution.py:433
  32.7 0.0 collective-permute-done.6.halo
  32.8 9.8 %tiles1.1 = (bf16[2048,2048]{1,0:T(8,128)(2,1)S(1)}, bf16[2048,2048]{1,0:T(8,128)(2,1)S(1)}, f32[32,2048]{1,0:T(8,128)S(1)}) custom-call(s32[4]{0:T(128)S(1)} %pad_add_fusion.place, f32[8,128]{1,0:T(8,128)S(1)} %get-tuple-element.36.own, f32[40,2176]{1,0:T(8,128)S(1)} %collective-permute-done.6.halo, f32[8,2048]{1,0:T(8,128)S(1)} %get-tuple-element.38.first, ...), custom_call_target="tpu_custom_call" | custom-call | tf_op jit(solution)/shard_map/tiles1/pallas_call | solution.py:381
  42.6 0.0 collective-permute-done.5.halo
  42.6 9.8 %tiles2.1 = (bf16[2048,2048]{1,0:T(8,128)(2,1)S(1)}, bf16[2048,2048]{1,0:T(8,128)(2,1)S(1)}, f32[32,2048]{1,0:T(8,128)S(1)}) custom-call(s32[4]{0:T(128)S(1)} %pad_add_fusion.place, f32[8,128]{1,0:T(8,128)S(1)} %get-tuple-element.36.own, f32[40,2176]{1,0:T(8,128)S(1)} %collective-permute-done.5.halo, f32[8,2048]{1,0:T(8,128)S(1)} %get-tuple-element.38.first, ...), custom_call_target="tpu_custom_call" | custom-call | tf_op jit(solution)/shard_map/tiles2/pallas_call | solution.py:381
  52.4 0.0 collective-permute-done.4.halo
  52.4 4.7 %tiles3.1 = (bf16[7168,256]{1,0:T(8,128)(2,1)S(1)}, bf16[7168,256]{1,0:T(8,128)(2,1)S(1)}, f32[32,2048]{1,0:T(8,128)S(1)}) custom-call(s32[4]{0:T(128)S(1)} %pad_add_fusion.place, f32[8,128]{1,0:T(8,128)S(1)} %get-tuple-element.36.own, f32[40,2176]{1,0:T(8,128)S(1)} %collective-permute-done.4.halo, f32[8,2048]{1,0:T(8,128)S(1)} %get-tuple-element.38.first, ...), custom_call_target="tpu_custom_call" | custom-call | tf_op jit(solution)/shard_map/tiles3/pallas_call | solution.py:410
  57.1 0.4 collective-permute-start.7
  57.5 1.2 %collective-permute-done.7.other = f32[32,2048]{1,0:T(8,128)S(1)} collective-permute-done((f32[32,2048]{1,0:T(8,128)S(1)}, f32[32,2048]{1,0:T(8,128)S(1)}, u32[]{:S(2)}, u32[]{:S(2)}) %collective-permute-start.7) | collective-permute-done | bytes 262176 | tf_op jit(solution)/shard_map/ppermute | solution.py:602
  58.7 0.1 combine.1
  58.7 2.1 %collective-permute-start.10 = (f32[32,2048]{1,0:T(8,128)S(1)}, f32[32,2048]{1,0:T(8,128)S(1)}, u32[]{:S(2)}, u32[]{:S(2)}) collective-permute-start(f32[32,2048]{1,0:T(8,128)S(1)} %get-tuple-element.46.vector), channel_id=1, source_target_pairs={{2,0},{1,3},{6,2},{3,7},{4,6},{7,5},{12,4},{5,13},{14,12},{13,15},... | collective-permute-start | bytes 786440 | tf_op jit(solution)/shard_map/ppermute | solution.py:597
  60.8 4.9 %collective-permute-start.9 = (f32[32,2048]{1,0:T(8,128)S(1)}, f32[32,2048]{1,0:T(8,128)S(1)}, u32[]{:S(2)}, u32[]{:S(2)}) collective-permute-start(f32[32,2048]{1,0:T(8,128)S(1)} %get-tuple-element.46.vector), channel_id=1, source_target_pairs={{6,0},{1,7},{4,2},{3,5},{12,6},{7,13},{14,4},{5,15},{10,12},{13,11... | collective-permute-start | bytes 786440 | tf_op jit(solution)/shard_map/ppermute | solution.py:597
  65.7 4.9 %collective-permute-start.8 = (f32[32,2048]{1,0:T(8,128)S(1)}, f32[32,2048]{1,0:T(8,128)S(1)}, u32[]{:S(2)}, u32[]{:S(2)}) collective-permute-start(f32[32,2048]{1,0:T(8,128)S(1)} %get-tuple-element.46.vector), channel_id=1, source_target_pairs={{4,0},{1,5},{12,2},{3,13},{14,6},{7,15},{10,4},{5,11},{8,12},{13,9... | collective-permute-start | bytes 786440 | tf_op jit(solution)/shard_map/ppermute | solution.py:597
  70.6 1.5 %apply.5.before = f32[32,2048]{1,0:T(8,128)S(1)} custom-call(f32[32,2048]{1,0:T(8,128)S(1)} %get-tuple-element.46.vector, bf16[1024,2048]{1,0:T(8,128)(2,1)S(1)} %get-tuple-element.40.high, bf16[1024,2048]{1,0:T(8,128)(2,1)S(1)} %get-tuple-element.41.low, f32[32,2048]{1,0:T(8,128)S(1)} %broadcast_1_before.2.before), custom_call_target="tpu_custom_call" | custom-call | tf_op jit(solution)/shard_map/apply/pallas_call | solution.py:433
  72.1 0.0 collective-permute-done.10.vector
  72.1 3.0 %apply.6.before = f32[32,2048]{1,0:T(8,128)S(1)} custom-call(f32[32,2048]{1,0:T(8,128)S(1)} %collective-permute-done.10.vector, bf16[2048,2048]{1,0:T(8,128)(2,1)S(1)} %get-tuple-element.51.high, bf16[2048,2048]{1,0:T(8,128)(2,1)S(1)} %get-tuple-element.52.low, f32[32,2048]{1,0:T(8,128)S(1)} %apply.5.before), custom_call_target="tpu_custom_call" | custom-call | tf_op jit(solution)/shard_map/apply/pallas_call | solution.py:433
  75.2 0.0 collective-permute-done.9.vector
  75.2 3.0 %apply.7.before = f32[32,2048]{1,0:T(8,128)S(1)} custom-call(f32[32,2048]{1,0:T(8,128)S(1)} %collective-permute-done.9.vector, bf16[2048,2048]{1,0:T(8,128)(2,1)S(1)} %get-tuple-element.49.high, bf16[2048,2048]{1,0:T(8,128)(2,1)S(1)} %get-tuple-element.50.low, f32[32,2048]{1,0:T(8,128)S(1)} %apply.6.before), custom_call_target="tpu_custom_call" | custom-call | tf_op jit(solution)/shard_map/apply/pallas_call | solution.py:433
  78.2 0.0 copy-start
  78.2 0.2 collective-permute-done.8.vector
  78.4 1.3 %apply3.1.mine = f32[32,2048]{1,0:T(8,128)S(1)} custom-call(f32[32,2048]{1,0:T(8,128)S(1)} %collective-permute-done.8.vector, bf16[7168,256]{1,0:T(8,128)(2,1)S(1)} %get-tuple-element.47.high, bf16[7168,256]{1,0:T(8,128)(2,1)S(1)} %get-tuple-element.48.low, f32[32,2048]{1,0:T(8,128)S(1)} %apply.7.before), custom_call_target="tpu_custom_call" | custom-call | tf_op jit(solution)/shard_map/apply3/pallas_call | solution.py:456
  79.7 0.0 collective-permute-start.11
  79.8 1.5 %collective-permute-done.11.other = f32[32,2048]{1,0:T(8,128)S(1)} collective-permute-done((f32[32,2048]{1,0:T(8,128)S(1)}, f32[32,2048]{1,0:T(8,128)S(1)}, u32[]{:S(2)}, u32[]{:S(2)}) %collective-permute-start.11) | collective-permute-done | bytes 262176 | tf_op jit(solution)/shard_map/ppermute | solution.py:602
  81.3 0.8 finish.1
  82.1 1.2 %collective-permute-start.12 = (f32[4,4224]{1,0:T(4,128)S(1)}, f32[4,4224]{1,0:T(4,128)S(1)}, u32[]{:S(2)}, u32[]{:S(2)}) collective-permute-start(f32[4,4224]{1,0:T(4,128)S(1)} %get-tuple-element.55), channel_id=1, source_target_pairs={{0,2},{1,3},{2,4},{3,5},{4,6},{5,7},{6,0},{7,1},{8,10},{9,11},{10,... | collective-permute-start | bytes 202760 | tf_op jit(solution)/shard_map/ppermute | solution.py:611
  83.3 3.0 %collective-permute-start.13 = (f32[4,4224]{1,0:T(4,128)S(1)}, f32[4,4224]{1,0:T(4,128)S(1)}, u32[]{:S(2)}, u32[]{:S(2)}) collective-permute-start(f32[4,4224]{1,0:T(4,128)S(1)} %get-tuple-element.56), channel_id=1, source_target_pairs={{0,4},{1,5},{2,6},{3,7},{4,0},{5,1},{6,2},{7,3},{8,12},{9,13},{10,... | collective-permute-start | bytes 202760 | tf_op jit(solution)/shard_map/ppermute | solution.py:611
  86.3 1.7 %collective-permute-start.14 = (f32[4,4224]{1,0:T(4,128)S(1)}, f32[4,4224]{1,0:T(4,128)S(1)}, u32[]{:S(2)}, u32[]{:S(2)}) collective-permute-start(f32[4,4224]{1,0:T(4,128)S(1)} %get-tuple-element.57), channel_id=1, source_target_pairs={{0,6},{1,7},{2,0},{3,1},{4,2},{5,3},{6,4},{7,5},{8,14},{9,15},{10,... | collective-permute-start | bytes 202760 | tf_op jit(solution)/shard_map/ppermute | solution.py:611
  88.0 0.0 collective-permute-done.12.behind1
  88.0 1.8 %collective-permute-done.13.behind2 = f32[4,4224]{1,0:T(4,128)S(1)} collective-permute-done((f32[4,4224]{1,0:T(4,128)S(1)}, f32[4,4224]{1,0:T(4,128)S(1)}, u32[]{:S(2)}, u32[]{:S(2)}) %collective-permute-start.13) | collective-permute-done | bytes 67616 | tf_op jit(solution)/shard_map/ppermute | solution.py:611
  89.9 0.7 collective-permute-done.14.behind3
  90.6 19.7 %all_to_all.5.sums = f32[32,4,128]{2,1,0:T(4,128)S(1)} all-to-all(f32[32,4,128]{2,1,0:T(4,128)S(1)} %region_sums.1), channel_id=1, replica_groups=mesh['region'=32,'cols'=8] {'region'}, dimensions={0} | all-to-all | bytes 131072 | tf_op jit(solution)/shard_map/all_to_all | solution.py:659
  110.2 0.0 copy-done
  110.2 1.5 %result.1 = (f32[4,8192]{1,0:T(4,128)}, f32[4,8192]{1,0:T(4,128)}) custom-call(s32[4]{0:T(128)S(1)} %pad_add_fusion.place, f32[32,4,128]{2,1,0:T(4,128)S(1)} %all_to_all.5.sums, f32[4,8192]{1,0:T(4,128)S(1)} %copy-done, f32[4,4224]{1,0:T(4,128)S(1)} %get-tuple-element.54.own, f32[4,4224]{1,0:T(4,128)S(1)} %collective-permute-done.12.behind1, ...), custom_call_target="tpu_custom_call" | custom-call | tf_op jit(solution)/shard_map/result/pallas_call | solution.py:577
  (2 shorter events, 0.0 us)
Async XLA Ops:
  2.8 5.9 %collective-permute-start = (f32[4,2176]{1,0:T(4,128)S(1)}, f32[4,2176]{1,0:T(4,128)S(1)}, u32[]{:S(2)}, u32[]{:S(2)}) collective-permute-start(f32[4,2176]{1,0:T(4,128)S(1)} %get-tuple-element.31), channel_id=1, source_target_pairs={{0,2},{1,3},{2,4},{3,5},{4,6},{5,7},{6,0},{7,1},{8,10},{9,11},{10,... | collective-permute-start | bytes 104456 | tf_op jit(solution)/shard_map/ppermute | solution.py:611
  4.5 5.4 %collective-permute-start.1 = (f32[4,2176]{1,0:T(4,128)S(1)}, f32[4,2176]{1,0:T(4,128)S(1)}, u32[]{:S(2)}, u32[]{:S(2)}) collective-permute-start(f32[4,2176]{1,0:T(4,128)S(1)} %get-tuple-element.32), channel_id=1, source_target_pairs={{0,4},{1,5},{2,6},{3,7},{4,0},{5,1},{6,2},{7,3},{8,12},{9,13},{10,... | collective-permute-start | bytes 104456 | tf_op jit(solution)/shard_map/ppermute | solution.py:611
  7.4 3.9 %collective-permute-start.2 = (f32[4,2176]{1,0:T(4,128)S(1)}, f32[4,2176]{1,0:T(4,128)S(1)}, u32[]{:S(2)}, u32[]{:S(2)}) collective-permute-start(f32[4,2176]{1,0:T(4,128)S(1)} %get-tuple-element.33), channel_id=1, source_target_pairs={{0,6},{1,7},{2,0},{3,1},{4,2},{5,3},{6,4},{7,5},{8,14},{9,15},{10,... | collective-permute-start | bytes 104456 | tf_op jit(solution)/shard_map/ppermute | solution.py:611
  11.9 2.2 %collective-permute-start.3 = (f32[16,2176]{1,0:T(8,128)S(1)}, f32[16,2176]{1,0:T(8,128)S(1)}, u32[]{:S(2)}, u32[]{:S(2)}) collective-permute-start(f32[16,2176]{1,0:T(8,128)S(1)} %assemble.1.mine), channel_id=1, source_target_pairs={{0,1},{1,0},{2,3},{3,2},{4,5},{5,4},{6,7},{7,6},{8,9},{9,8},{10,11... | collective-permute-start | bytes 417800 | tf_op jit(solution)/shard_map/ppermute | solution.py:602
  12.0 0.7 copy-start.1
  15.0 17.8 %collective-permute-start.6 = (f32[40,2176]{1,0:T(8,128)S(1)}, f32[40,2176]{1,0:T(8,128)S(1)}, u32[]{:S(2)}, u32[]{:S(2)}) collective-permute-start(f32[40,2176]{1,0:T(8,128)S(1)} %get-tuple-element.37.halo.vector), channel_id=1, source_target_pairs={{2,0},{1,3},{6,2},{3,7},{4,6},{7,5},{12,4},{5,13},{14,12},{13,15},... | collective-permute-start | bytes 1044488 | tf_op jit(solution)/shard_map/ppermute | solution.py:597
  17.1 25.5 %collective-permute-start.5 = (f32[40,2176]{1,0:T(8,128)S(1)}, f32[40,2176]{1,0:T(8,128)S(1)}, u32[]{:S(2)}, u32[]{:S(2)}) collective-permute-start(f32[40,2176]{1,0:T(8,128)S(1)} %get-tuple-element.37.halo.vector), channel_id=1, source_target_pairs={{6,0},{1,7},{4,2},{3,5},{12,6},{7,13},{14,4},{5,15},{10,12},{13,11... | collective-permute-start | bytes 1044488 | tf_op jit(solution)/shard_map/ppermute | solution.py:597
  21.4 31.0 %collective-permute-start.4 = (f32[40,2176]{1,0:T(8,128)S(1)}, f32[40,2176]{1,0:T(8,128)S(1)}, u32[]{:S(2)}, u32[]{:S(2)}) collective-permute-start(f32[40,2176]{1,0:T(8,128)S(1)} %get-tuple-element.37.halo.vector), channel_id=1, source_target_pairs={{4,0},{1,5},{12,2},{3,13},{14,6},{7,15},{10,4},{5,11},{8,12},{13,9... | collective-permute-start | bytes 1044488 | tf_op jit(solution)/shard_map/ppermute | solution.py:597
  57.1 1.6 %collective-permute-start.7 = (f32[32,2048]{1,0:T(8,128)S(1)}, f32[32,2048]{1,0:T(8,128)S(1)}, u32[]{:S(2)}, u32[]{:S(2)}) collective-permute-start(f32[32,2048]{1,0:T(8,128)S(1)} %get-tuple-element.44.mine), channel_id=1, source_target_pairs={{0,1},{1,0},{2,3},{3,2},{4,5},{5,4},{6,7},{7,6},{8,9},{9,8},{10,11... | collective-permute-start | bytes 786440 | tf_op jit(solution)/shard_map/ppermute | solution.py:602
  58.7 13.4 %collective-permute-start.10 = (f32[32,2048]{1,0:T(8,128)S(1)}, f32[32,2048]{1,0:T(8,128)S(1)}, u32[]{:S(2)}, u32[]{:S(2)}) collective-permute-start(f32[32,2048]{1,0:T(8,128)S(1)} %get-tuple-element.46.vector), channel_id=1, source_target_pairs={{2,0},{1,3},{6,2},{3,7},{4,6},{7,5},{12,4},{5,13},{14,12},{13,15},... | collective-permute-start | bytes 786440 | tf_op jit(solution)/shard_map/ppermute | solution.py:597
  60.8 14.4 %collective-permute-start.9 = (f32[32,2048]{1,0:T(8,128)S(1)}, f32[32,2048]{1,0:T(8,128)S(1)}, u32[]{:S(2)}, u32[]{:S(2)}) collective-permute-start(f32[32,2048]{1,0:T(8,128)S(1)} %get-tuple-element.46.vector), channel_id=1, source_target_pairs={{6,0},{1,7},{4,2},{3,5},{12,6},{7,13},{14,4},{5,15},{10,12},{13,11... | collective-permute-start | bytes 786440 | tf_op jit(solution)/shard_map/ppermute | solution.py:597
  65.7 12.7 %collective-permute-start.8 = (f32[32,2048]{1,0:T(8,128)S(1)}, f32[32,2048]{1,0:T(8,128)S(1)}, u32[]{:S(2)}, u32[]{:S(2)}) collective-permute-start(f32[32,2048]{1,0:T(8,128)S(1)} %get-tuple-element.46.vector), channel_id=1, source_target_pairs={{4,0},{1,5},{12,2},{3,13},{14,6},{7,15},{10,4},{5,11},{8,12},{13,9... | collective-permute-start | bytes 786440 | tf_op jit(solution)/shard_map/ppermute | solution.py:597
  78.2 32.0 %copy-start = (f32[4,8192]{1,0:T(4,128)S(1)}, f32[4,8192]{1,0:T(4,128)}, u32[]{:S(2)}) copy-start(f32[4,8192]{1,0:T(4,128)} %innovations.3) | copy-start | bytes 393220
  79.7 1.6 %collective-permute-start.11 = (f32[32,2048]{1,0:T(8,128)S(1)}, f32[32,2048]{1,0:T(8,128)S(1)}, u32[]{:S(2)}, u32[]{:S(2)}) collective-permute-start(f32[32,2048]{1,0:T(8,128)S(1)} %apply3.1.mine), channel_id=1, source_target_pairs={{0,1},{1,0},{2,3},{3,2},{4,5},{5,4},{6,7},{7,6},{8,9},{9,8},{10,11... | collective-permute-start | bytes 786440 | tf_op jit(solution)/shard_map/ppermute | solution.py:602
  82.1 5.9 %collective-permute-start.12 = (f32[4,4224]{1,0:T(4,128)S(1)}, f32[4,4224]{1,0:T(4,128)S(1)}, u32[]{:S(2)}, u32[]{:S(2)}) collective-permute-start(f32[4,4224]{1,0:T(4,128)S(1)} %get-tuple-element.55), channel_id=1, source_target_pairs={{0,2},{1,3},{2,4},{3,5},{4,6},{5,7},{6,0},{7,1},{8,10},{9,11},{10,... | collective-permute-start | bytes 202760 | tf_op jit(solution)/shard_map/ppermute | solution.py:611
  83.3 6.6 %collective-permute-start.13 = (f32[4,4224]{1,0:T(4,128)S(1)}, f32[4,4224]{1,0:T(4,128)S(1)}, u32[]{:S(2)}, u32[]{:S(2)}) collective-permute-start(f32[4,4224]{1,0:T(4,128)S(1)} %get-tuple-element.56), channel_id=1, source_target_pairs={{0,4},{1,5},{2,6},{3,7},{4,0},{5,1},{6,2},{7,3},{8,12},{9,13},{10,... | collective-permute-start | bytes 202760 | tf_op jit(solution)/shard_map/ppermute | solution.py:611
  86.3 4.3 %collective-permute-start.14 = (f32[4,4224]{1,0:T(4,128)S(1)}, f32[4,4224]{1,0:T(4,128)S(1)}, u32[]{:S(2)}, u32[]{:S(2)}) collective-permute-start(f32[4,4224]{1,0:T(4,128)S(1)} %get-tuple-element.57), channel_id=1, source_target_pairs={{0,6},{1,7},{2,0},{3,1},{4,2},{5,3},{6,4},{7,5},{8,14},{9,15},{10,... | collective-permute-start | bytes 202760 | tf_op jit(solution)/shard_map/ppermute | solution.py:611
